TPU v7x, 128 devices: a whole 4x4x4 slice. The times are simulated.
128 devices in a mesh: rep: 16 (over y, z_lo, core), shard: 8 (over z_hi, x).
Axes of the slice: x: 4, y: 4, z: 4 (z_hi: 2, z_lo: 2; z = z_hi * 2 + z_lo), core: 2. Of those that a mesh axis runs over, the one named last changes fastest.
Arguments:
- tokens: bfloat16 [24576, 1152], P(('rep', 'shard')), may hold values from -6 to 6
- lengths: int32 [16, 8], P('rep', 'shard'), may hold values from 128 to 192, as said below
- attn_gain: bfloat16 [1152], P('shard'), may hold values from 0.25 to 1.75
- w_query: bfloat16 [1152, 1024], P('shard'), may hold values from -0.1875 to 0.1875
- w_keyval: bfloat16 [1152, 512], P('shard'), may hold values from -0.1875 to 0.1875
- w_out: bfloat16 [1024, 1152], P('shard'), may hold values from -1.5 to 1.5
- mlp_gain: bfloat16 [1152], P('shard'), may hold values from 0.25 to 1.75
- w_gate: bfloat16 [1152, 6912], P('shard'), may hold values from -0.1875 to 0.1875
- w_up: bfloat16 [1152, 6912], P('shard'), may hold values from -0.1875 to 0.1875
- w_down: bfloat16 [6912, 1152], P('shard'), may hold values from -0.15625 to 0.15625
- cotangent: bfloat16 [24576, 1152], P(('rep', 'shard')), may hold values from -6 to 6
Outputs:
- outputs: bfloat16 [24576, 1152], P(('rep', 'shard'))
- grad_tokens: float32 [24576, 1152], P(('rep', 'shard'))
- grad_attn_gain: float32 [1152], P('shard')
- grad_w_query: float32 [1152, 1024], P('shard')
- grad_w_keyval: float32 [1152, 512], P('shard')
- grad_w_out: float32 [1024, 1152], P('shard')
- grad_mlp_gain: float32 [1152], P('shard')
- grad_w_gate: float32 [1152, 6912], P('shard')
- grad_w_up: float32 [1152, 6912], P('shard')
- grad_w_down: float32 [6912, 1152], P('shard')
Inputs may be any that keep to these rules, and one draw needn't show every extreme that they name: lengths[r, s] counts the live slots at the start of the 192 slots of shard index s in sequence r; in every sequence one device has all 192 live and another has exactly 128.
All inputs are finite; a program needn't handle non-finite values.
Results may differ from a plain program's by a relative error of at most 0.025.
Values may be sent and summed in bfloat16 or wider, within the bound.
A program may use at most 256 MiB of HBM per device.

v0:
```python
import functools

import jax
import jax.numpy as jnp
import numpy as np
from jax import lax
from jax.experimental import pallas as pl
from jax.experimental.pallas import tpu as pltpu
from jax.sharding import PartitionSpec as P

MESH = pl.DeviceIdType.MESH
WINDOW = 512
EPSILON = 1e-06
MASKED = -1e30
VMEM_LIMIT = 60 * 2**20
FF_DEV = 864
FF_PAD = 896
PAIRS = FF_PAD // 128
BEHIND = 4


def matmul(former, latter):
    return jnp.dot(former, latter, preferred_element_type=jnp.float32)


def lead_product(former, latter):
    return lax.dot_general(
        former, latter, (((0,), (0,)), ((), ())), preferred_element_type=jnp.float32
    )


def trail_product(former, latter):
    return lax.dot_general(
        former, latter, (((1,), (1,)), ((), ())), preferred_element_type=jnp.float32
    )


class Place:
    def __init__(self):
        rep, shard = lax.axis_index("rep"), lax.axis_index("shard")
        self.rep, self.shard = rep, shard
        self.y, self.z_lo, self.core = rep // 4, (rep // 2) % 2, rep % 2
        self.z_hi, self.x = shard // 4, shard % 4

    def device(self, dx=0, dy=0, mirror=0, swap_lo=0, sibling=0):
        z_lo = (self.z_lo + mirror + swap_lo) % 2
        rep = (((self.y + dy) % 4) * 2 + z_lo) * 2 + (self.core + sibling) % 2
        return (rep, ((self.z_hi + mirror) % 2) * 4 + (self.x + dx) % 4)

    def over_group(self, dx, mirror):
        return self.device(dx=dx, mirror=mirror)

    def shard_at(self, j, p):
        return ((self.z_hi + p) % 2) * 4 + (self.x + STEPS[j]) % 4


STEPS = (0, 1, 3, 2)


class Wire:
    def __init__(self, send_sems, recv_sems):
        self.send_sems, self.recv_sems, self.made = send_sems, recv_sems, []

    def copy(self, src, dst, device):
        k = len(self.made)
        made = pltpu.make_async_remote_copy(
            src_ref=src,
            dst_ref=dst,
            send_sem=self.send_sems.at[k],
            recv_sem=self.recv_sems.at[k],
            device_id=device,
            device_id_type=MESH,
        )
        self.made.append(made)
        return made

    def drain(self):
        for made in self.made:
            made.wait_send()


def greet(devices):
    barrier = pltpu.get_barrier_semaphore()
    for device in devices:
        pl.semaphore_signal(barrier, inc=1, device_id=device, device_id_type=MESH)
    pl.semaphore_wait(barrier, len(devices))


HOPS = (
    ((0, 0), (0, 1), 1, 0, 1),
    ((0, 0), (0, 1), 2, 0, 1),
    ((0, 0), (2, 0), 1, 1, 0),
    ((0, 0), (2, 0), 2, 1, 0),
    ((0, 0), (1, 0), 1, 3, 0),
    ((0, 0), (1, 0), 2, 3, 0),
    ((0, 1), (2, 1), 1, 1, 0),
    ((0, 1), (1, 1), 1, 3, 0),
    ((2, 0), (3, 0), 1, 1, 0),
    ((1, 0), (3, 0), 2, 3, 0),
    ((2, 0), (2, 1), 2, 0, 1),
    ((1, 0), (1, 1), 2, 0, 1),
    ((2, 1), (3, 1), 1, 1, 0),
    ((1, 1), (3, 1), 2, 3, 0),
)
FIRST = (0, 2, 5, 1, 3, 4)
ONWARD = {0: (6, 7), 2: (8,), 3: (10,), 5: (9, 11), 6: (12,), 11: (13,)}
SERVE = (0, 2, 5, 3, 11, 6, 1, 4, 7, 8, 9, 10, 12, 13)
WHOLE = {1: (0, 1), 3: (2, 0), 4: (1, 0), 7: (1, 1), 9: (3, 0), 10: (2, 1), 13: (3, 1)}
HOPS_FAR = tuple(HOPS[k] for k in (13, 12, 9, 8))
RING = (
    ((0, 0), (2, 0), 0, 1, 0),
    ((0, 0), (1, 0), 0, 3, 0),
    ((2, 0), (3, 0), 1, 1, 0),
    ((1, 0), (3, 0), 2, 3, 0),
)
RING_ONWARD = {0: (2,), 1: (3,)}


def gather_tree(wire, device_of, hops, own, slot, cut, absolute):
    copies = []
    for source, target, part, dx, mirror in hops:
        src = own if source == (0, 0) else slot(*source)
        dst = slot(*(source if absolute else target))
        copies.append(wire.copy(cut(src, part), cut(dst, part), device_of(dx, mirror)))
    return copies


def arrive(tree, k, after=ONWARD):
    tree[k].wait_recv()
    for n in after.get(k, ()):
        tree[n].start()


def add_into(target, source):
    target[...] = (target[...].astype(jnp.float32) + source[...].astype(jnp.float32)).astype(
        target.dtype
    )


class SumTree:
    def __init__(self, wire, device_of, hops, slot, cut, landings):
        self.hops, self.slot, self.cut, self.landings = hops, slot, cut, landings
        self.copies = [
            wire.copy(cut(slot(*target), part), landing, device_of((4 - dx) % 4, mirror))
            for (_, target, part, dx, mirror), landing in zip(hops, landings)
        ]

    def start(self, *hops):
        for k in hops:
            self.copies[k].start()

    def absorb(self, *hops):
        for k in hops:
            source, _, part, _, _ = self.hops[k]
            self.copies[k].wait_recv()
            add_into(self.cut(self.slot(*source), part), self.landings[k])

    def send_far(self):
        self.start(13, 12, 9, 8)

    def send_mid(self):
        self.start(7, 4, 10)

    def send_near(self):
        self.absorb(13)
        self.start(11)
        self.absorb(12)
        self.start(6)
        self.absorb(8)
        self.start(2)

    def send_next(self):
        self.absorb(9, 11)
        self.start(5)
        self.absorb(10)
        self.start(3)

    def send_last(self):
        self.absorb(6, 7)
        self.start(0)

    def finish(self, axis):
        halves = []
        for part in (1, 2):
            total = self.cut(self.slot(0, 0), part)[...].astype(jnp.float32)
            for k in (4, 2, 0):
                self.copies[k + part - 1].wait_recv()
                total = total + self.landings[k + part - 1][...].astype(jnp.float32)
            halves.append(total)
        return jnp.concatenate(halves, axis=axis)


def front_kernel(
    tokens, cot, misc, freq, w_query, w_keyval, w_out, w_gate, w_up,
    o_misc, o_qkv, o_wo, o_gu, o_gb, o_normed1, o_q, o_kv, o_probs, o_att, o_middle, o_normed2, o_rope,
    x_ref, cot_ref, miscs, freq_ref, wqkv, wo, gate, up, packed, gb_own, normed1, q_ref, kv_ref,
    bias, probs, att, middle, normed2, rope,
    local_sems, send_sems, recv_sems,
):
    place = Place()
    wire = Wire(send_sems, recv_sems)
    core, me, y = place.core, place.shard, place.y
    rows, width = tokens.shape
    at = place.shard_at
    others = [(j, p) for p in (0, 1) for j in range(4) if (j, p) != (0, 0)]
    group = [place.device(dx=STEPS[j], mirror=p) for j, p in others]
    sequence = [(place.rep, at(j, p)) for j, p in others]
    sibling = place.device(sibling=1)
    column = [place.device(dy=d) for d in (1, 3, 2)]
    locals_ = []

    def local(src, dst):
        copy = pltpu.make_async_copy(src, dst, local_sems.at[len(locals_)])
        copy.start()
        locals_.append(copy)
        return copy

    load_x = local(tokens, x_ref)
    load_cot = local(cot, cot_ref)
    load_misc = local(misc, miscs.at[me])
    load_freq = local(freq, freq_ref)
    load_gate = local(w_gate, gate)
    load_up = local(w_up, up)
    load_own = [
        local(w_query, wqkv.at[me, :, pl.ds(0, 1024)]),
        local(w_keyval, wqkv.at[me, :, pl.ds(1024, 512)]),
        local(w_out, wo.at[me]),
    ]
    greet([sibling] + group + [d for d, (j, p) in zip(sequence, others) if p == 1] + column)

    def lanes_from(base, size):
        def cut(ref, part):
            start, count = ((0, size), (0, size // 2), (size // 2, size // 2))[part]
            start = pl.multiple_of(core * size + (base + start), 128)
            return ref.at[:, pl.ds(start, count)]

        return cut

    def cut_wo(ref, part):
        start, size = ((0, 64), (0, 32), (32, 32))[part]
        return ref.at[pl.ds(pl.multiple_of(core * 64 + start, 32), size)]

    def cut_gb(ref, part):
        return ref if part == 0 else ref.at[pl.ds((part - 1) * 96, 96)]

    def cut_gu(ref):
        return ref.at[:, pl.ds(pl.multiple_of(core * FF_PAD, 128), FF_PAD)]

    cut_q, cut_kv = lanes_from(0, 512), lanes_from(1024, 256)
    slot_qkv = lambda j, p: wqkv.at[at(j, p)]
    slot_wo = lambda j, p: wo.at[at(j, p)]
    slot_gb = lambda j, p: o_gb.at[j, p]
    misc_copies = [wire.copy(misc, miscs.at[me], device) for device in sequence]
    for copy in misc_copies:
        copy.start()
    for load in load_own:
        load.wait()
    own = wqkv.at[me]
    trees = [
        gather_tree(wire, place.over_group, HOPS, own, slot_qkv, cut_q, True),
        gather_tree(wire, place.over_group, HOPS, own, slot_qkv, cut_kv, True),
        gather_tree(wire, place.over_group, HOPS, wo.at[me], slot_wo, cut_wo, True),
    ]
    cuts = [cut_q, cut_kv, cut_wo]
    slots = [slot_qkv, slot_qkv, slot_wo]
    passes = [
        {k: wire.copy(cut(slot(*jp), 0), cut(slot(*jp), 0), sibling) for k, jp in WHOLE.items()}
        for cut, slot in zip(cuts, slots)
    ]
    for tree in trees:
        for k in FIRST:
            tree[k].start()

    load_x.wait()
    inputs = x_ref[...].astype(jnp.float32)
    inverse1 = lax.rsqrt(jnp.mean(inputs * inputs, axis=1, keepdims=True) + EPSILON)
    middle[...] = inputs * inverse1
    load_gate.wait()
    load_up.wait()
    for d in range(8):
        for t in range(PAIRS):
            start = FF_DEV * d + 128 * t
            size = min(128, FF_DEV - 128 * t)
            for k, weight in enumerate((gate, up)):
                block = weight[:, start : start + size]
                if size < 128:
                    block = jnp.concatenate(
                        [block, jnp.zeros((block.shape[0], 128 - size), block.dtype)], axis=1
                    )
                packed[d, :, 256 * t + 128 * k : 256 * t + 128 * (k + 1)] = block

    def attn(*hops):
        for k in hops:
            for tree, onward in zip(trees, passes):
                arrive(tree, k)
                if k in onward:
                    onward[k].start()

    z_of = lambda p: (place.z_hi + p) % 2
    shard_from = lambda d, p: z_of(p) * 4 + (place.x + y + d) % 4
    turn = []
    for p in (0, 1):
        target = z_of(p) * 4 + (place.x - y + 4) % 4
        turn.append(
            wire.copy(
                cut_gu(packed.at[target]), cut_gu(o_gu.at[me]), place.device(dx=4 - y, mirror=p)
            )
        )
    away, home = y > 0, y == 0
    keep_own = pltpu.make_async_copy(
        cut_gu(packed.at[me]), cut_gu(o_gu.at[me]), local_sems.at[len(locals_)]
    )
    locals_.append(None)
    turn[1].start()
    pl.when(away)(turn[0].start)
    pl.when(home)(keep_own.start)

    def over_y(dx, mirror):
        return place.device(dy=dx)

    def cut_block(ref, part):
        start, size = ((0, 144), (0, 80), (80, 64))[part]
        return ref.at[pl.ds(start, size), pl.ds(pl.multiple_of(core * FF_PAD, 128), FF_PAD)]

    gu_slots = [lambda j, _, p=p: o_gu.at[shard_from(STEPS[j], p)] for p in (0, 1)]
    gu_trees = [
        gather_tree(wire, over_y, RING, slot(0, 0), slot, cut_block, True) for slot in gu_slots
    ]
    gu_passes = {
        (j, p): wire.copy(
            cut_gu(o_gu.at[shard_from(STEPS[j], p)]),
            cut_gu(o_gu.at[shard_from(STEPS[j], p)]),
            sibling,
        )
        for j in range(4)
        for p in (0, 1)
    }

    def over(k, j):
        for p in (0, 1):
            arrive(gu_trees[p], k, RING_ONWARD)
            if j:
                gu_passes[j, p].start()

    attn(0, 2, 5)
    load_cot.wait()
    load_misc.wait()
    load_freq.wait()
    live_col = (
        lax.broadcasted_iota(jnp.int32, (rows, 1), 0).astype(jnp.float32)
        < miscs[me].astype(jnp.float32)[2:3, :1]
    )
    gb_own[...] = jnp.where(live_col, cot_ref[...].astype(jnp.float32), 0.0).astype(jnp.bfloat16)
    gb_tree = gather_tree(wire, place.over_group, HOPS, gb_own, slot_gb, cut_gb, False)
    attn(3, 11, 6)
    pl.when(away)(turn[0].wait_recv)
    turn[1].wait_recv()
    pl.when(home)(keep_own.wait)
    for p in (0, 1):
        gu_trees[p][0].start()
        gu_trees[p][1].start()
        gu_passes[0, p].start()
    for k in FIRST:
        gb_tree[k].start()
    local(gb_own, o_gb.at[0, 0])
    attn(1, 4, 7, 8, 9, 10, 12, 13)

    for copy in misc_copies:
        copy.wait_recv()
    as_float = [miscs[s].astype(jnp.float32) for s in range(8)]
    gain1 = jnp.concatenate([m[0:1, :144] for m in as_float], axis=1)
    gain2 = jnp.concatenate([m[1:2, :144] for m in as_float], axis=1)
    normed = (middle[...] * gain1).astype(jnp.bfloat16)
    normed1[...] = normed
    for k in WHOLE:
        passes[0][k].wait_recv()
        passes[1][k].wait_recv()
    live = [m[2:3, :1] for m in as_float]
    start_of = []
    for i in range(BEHIND + 1):
        total = jnp.zeros((1, 1), jnp.float32)
        for s in range(8):
            total = total + jnp.where(s < me - i, 1.0, 0.0) * live[s]
        start_of.append(total)
    row = lax.broadcasted_iota(jnp.int32, (rows, 1), 0).astype(jnp.float32)
    query_pos = start_of[0] + row
    angles = query_pos * freq_ref[0:1, :]
    cosine, sine_part = jnp.cos(angles), jnp.sin(angles)
    rope[:, :128] = cosine
    rope[:, 128:] = sine_part
    weights = wqkv.reshape(width, 1536)

    def turned(vectors):
        first, second = vectors[:, :128], vectors[:, 128:]
        return jnp.concatenate(
            [first * cosine - second * sine_part, second * cosine + first * sine_part], axis=1
        )

    projected = matmul(normed, weights[:, 1024:1536])
    kv_ref[0, :, :256] = turned(projected[:, :256]).astype(jnp.bfloat16)
    kv_ref[0, :, 256:] = projected[:, 256:].astype(jnp.bfloat16)
    x, upper = place.x, place.z_hi == 1
    cross_kv = wire.copy(kv_ref.at[0], kv_ref.at[BEHIND], (place.rep, at(0, 1)))
    near_kv, far_kv = [], []
    for i in range(1, BEHIND):
        target = (place.rep, 4 * place.z_hi + (x + i) % 4)
        near_kv.append(wire.copy(kv_ref.at[0], kv_ref.at[i], target))
        far_kv.append(wire.copy(kv_ref.at[BEHIND], kv_ref.at[i], target))
    pl.when(jnp.logical_not(upper))(cross_kv.start)
    for i, copy in enumerate(near_kv):
        pl.when(x + (i + 1) < 4)(copy.start)
    for i in range(1, BEHIND + 1):

        @pl.when(me < i)
        def _():
            kv_ref[i] = jnp.zeros(kv_ref.shape[1:], kv_ref.dtype)

    def pass_kv():
        pl.when(upper)(cross_kv.wait_recv)
        for i, copy in enumerate(far_kv):
            pl.when(jnp.logical_and(upper, x + (i + 1) > 3))(copy.start)

    def have_kv():
        for i, (near, far) in enumerate(zip(near_kv, far_kv)):
            pl.when(x >= i + 1)(near.wait_recv)
            pl.when(jnp.logical_and(upper, x < i + 1))(far.wait_recv)

    scaling = 256 ** (-0.5)
    for h in range(4):
        heads = matmul(normed, weights[:, 256 * h : 256 * (h + 1)])
        q_ref[h] = (turned(heads) * scaling).astype(jnp.bfloat16)

    index = lax.broadcasted_iota(jnp.int32, (1, (BEHIND + 1) * rows), 1)
    key_pos = jnp.zeros(index.shape, jnp.float32)
    key_live = jnp.zeros(index.shape, jnp.float32)
    for i in range(BEHIND + 1):
        inside = jnp.logical_and(index >= i * rows, index < (i + 1) * rows)
        within = (index - i * rows).astype(jnp.float32)
        live_i = jnp.zeros((1, 1), jnp.float32)
        for s in range(8):
            live_i = live_i + jnp.where(me - i == s, 1.0, 0.0) * live[s]
        key_pos = jnp.where(inside, start_of[i] + within, key_pos)
        key_live = jnp.where(inside, jnp.where(within < live_i, 1.0, 0.0), key_live)
    ahead = query_pos - key_pos
    allowed = jnp.logical_and(
        jnp.logical_and(ahead >= 0.0, ahead < float(WINDOW)), key_live > 0.5
    )
    bias[...] = jnp.where(allowed, 0.0, MASKED)
    pass_kv()

    over(0, 2)
    over(1, 1)
    for k in SERVE[:4]:
        arrive(gb_tree, k)
    have_kv()
    all_kv = kv_ref.reshape((BEHIND + 1) * rows, 512)
    for h in range(4):
        scores = trail_product(q_ref[h], all_kv[:, :256]) + bias[...]
        raised = jnp.exp(scores - jnp.max(scores, axis=1, keepdims=True))
        share = raised * (1.0 / jnp.sum(raised, axis=1, keepdims=True))
        probs[h] = share
        att[:, 256 * h : 256 * (h + 1)] = matmul(
            share.astype(jnp.bfloat16), all_kv[:, 256:]
        ).astype(jnp.bfloat16)
        if h == 1:
            for k in SERVE[4:6]:
                arrive(gb_tree, k)
    for k in WHOLE:
        passes[2][k].wait_recv()
    keep = jnp.where(live_col, 1.0, 0.0)
    mid = x_ref[...].astype(jnp.float32) + keep * matmul(att[...], wo.reshape(1024, width)[...])
    middle[...] = mid
    inverse2 = lax.rsqrt(jnp.mean(mid * mid, axis=1, keepdims=True) + EPSILON)
    normed2[...] = (mid * inverse2 * gain2).astype(jnp.bfloat16)
    for src, dst in (
        (miscs, o_misc),
        (wqkv, o_qkv),
        (wo, o_wo),
        (normed1, o_normed1),
        (q_ref, o_q),
        (kv_ref, o_kv),
        (probs, o_probs),
        (att, o_att),
        (middle, o_middle),
        (normed2, o_normed2),
        (rope, o_rope),
    ):
        local(src, dst)
    over(2, 0)
    over(3, 3)
    for k in SERVE[6:]:
        arrive(gb_tree, k)
    for copy in gu_passes.values():
        copy.wait_recv()
    waited = [id(copy) for copy in near_kv + far_kv + [cross_kv, turn[0]]]
    for copy in locals_[9:]:
        if copy is not None:
            copy.wait()
    pl.when(away)(turn[0].wait_send)
    pl.when(jnp.logical_not(upper))(cross_kv.wait_send)
    for i, (near, far) in enumerate(zip(near_kv, far_kv)):
        pl.when(x + (i + 1) < 4)(near.wait_send)
        pl.when(jnp.logical_and(upper, x + (i + 1) > 3))(far.wait_send)
    for copy in wire.made:
        if id(copy) not in waited:
            copy.wait_send()


ANY = pl.BlockSpec(memory_space=pl.ANY)


def comm_params(collective_id):
    return pltpu.CompilerParams(
        collective_id=collective_id, has_side_effects=True, vmem_limit_bytes=VMEM_LIMIT
    )


def front(tokens, cot, misc, freq, w_query, w_keyval, w_out, w_gate, w_up):
    bf, f32 = jnp.bfloat16, jnp.float32
    rows, width = tokens.shape
    keys = (BEHIND + 1) * rows
    outs = [
        ((8, 16, 256), bf),
        ((8, 144, 1536), bf),
        ((8, 128, width), bf),
        ((8, 144, 2 * FF_PAD), bf),
        ((4, 2, rows, width), bf),
        ((rows, width), bf),
        ((4, rows, 256), bf),
        ((BEHIND + 1, rows, 512), bf),
        ((4, rows, keys), f32),
        ((rows, 1024), bf),
        ((rows, width), f32),
        ((rows, width), bf),
        ((rows, 256), f32),
    ]
    scratch = [
        ((rows, width), bf),
        ((rows, width), bf),
        ((8, 16, 256), bf),
        ((8, 128), f32),
        ((8, 144, 1536), bf),
        ((8, 128, width), bf),
        (w_gate.shape, bf),
        (w_up.shape, bf),
        ((8, 144, 2 * FF_PAD), bf),
        ((rows, width), bf),
        ((rows, width), bf),
        ((4, rows, 256), bf),
        ((BEHIND + 1, rows, 512), bf),
        ((rows, keys), f32),
        ((4, rows, keys), f32),
        ((rows, 1024), bf),
        ((rows, width), f32),
        ((rows, width), bf),
        ((rows, 256), f32),
    ]
    return pl.pallas_call(
        front_kernel,
        out_shape=tuple(jax.ShapeDtypeStruct(*o) for o in outs),
        in_specs=[ANY] * 9,
        out_specs=(ANY,) * len(outs),
        scratch_shapes=[pltpu.VMEM(*v) for v in scratch]
        + [
            pltpu.SemaphoreType.DMA((32,)),
            pltpu.SemaphoreType.DMA((136,)),
            pltpu.SemaphoreType.DMA((136,)),
        ],
        compiler_params=comm_params(1),
        name="attention_forward",
    )(tokens, cot, misc, freq, w_query, w_keyval, w_out, w_gate, w_up)


def finish_kernel(both, d_in, q_in, kv_in, wo_in, gate, up, d_out, q_out, kv_out, wo_out):
    for k, out in enumerate((gate, up)):
        parts = []
        for d in range(8):
            for t in range(PAIRS):
                half, q, first = (k, 3, 0) if t == 3 else (t // 4, t % 4, 128 * k)
                size = min(128, FF_DEV - 128 * t)
                parts.append(both[half, q, d, :, first : first + size])
        out[...] = jnp.concatenate(parts, axis=1).astype(jnp.float32)
    d_out[...] = d_in[...].astype(jnp.float32)
    q_out[...] = q_in[...].astype(jnp.float32)
    for c in range(2):
        for q in range(2):
            start = 256 * c + 128 * q
            kv_out[:, start : start + 128] = kv_in[c, q].astype(jnp.float32)

    @pl.when(pl.program_id(0) == 0)
    def _():
        wo_out[...] = wo_in[...].astype(jnp.float32)


def finish(both, d_in, q_in, kv_in, wo_in):
    rows, width = both.shape[3], d_in.shape[1]
    steps = rows // 16
    shapes = [(rows, 8 * FF_DEV)] * 2 + [(FF_DEV, width), (rows, 1024), (rows, 512), wo_in.shape]
    blocks = [(16, 8 * FF_DEV)] * 2 + [(FF_DEV // steps, width), (16, 1024), (16, 512)]
    by_row = lambda i: (i, 0)
    fixed = pl.BlockSpec(wo_in.shape, lambda i: (0, 0))
    return pl.pallas_call(
        finish_kernel,
        grid=(steps,),
        out_shape=[jax.ShapeDtypeStruct(shape, jnp.float32) for shape in shapes],
        in_specs=[
            pl.BlockSpec((2, 4, 8, 16, 256), lambda i: (0, 0, 0, i, 0)),
            pl.BlockSpec((FF_DEV // steps, width), by_row),
            pl.BlockSpec((16, 1024), by_row),
            pl.BlockSpec((2, 4, 16, 128), lambda i: (0, 0, i, 0)),
            fixed,
        ],
        out_specs=[pl.BlockSpec(block, by_row) for block in blocks] + [fixed],
        compiler_params=pltpu.CompilerParams(vmem_limit_bytes=VMEM_LIMIT),
        name="finish",
    )(both, d_in, q_in, kv_in, wo_in)


ROOT = 0.7978845608028654
CUBE = 0.044715


def ff_kernel(
    own_n, gb_all, wgu_all, wd_all,
    o_gn, o_pb, o_pgu, o_pd,
    nbuf, gb, wgu, wd, gh, hid, ggu, part_g, part_b, out_f32, dgu,
    g_half, dd, r_d, d_whole, d_half_a, d_half_b, z_d,
    r_gu, gu_half, n_turned, b_half,
    local_sems, send_sems, recv_sems,
):
    place = Place()
    wire = Wire(send_sems, recv_sems)
    loads = [
        pltpu.make_async_copy(src, dst, local_sems.at[k])
        for k, (src, dst) in enumerate(
            [(own_n, nbuf.at[0, 0]), (wd_all, wd.at[pl.ds(0, FF_DEV)]), (gb_all, gb), (wgu_all, wgu)]
        )
    ]
    for load in loads:
        load.start()
    core, y = place.core, place.y
    sibling, low = place.device(sibling=1), place.device(swap_lo=1)
    greet(
        [place.device(dx=1), place.device(dx=3), place.device(mirror=1), sibling, low]
        + [place.device(dy=1), place.device(dy=3)]
    )

    def cut(ref, part):
        return ref if part == 0 else ref.at[pl.ds((part - 1) * 96, 96)]

    slot_n = lambda j, p: nbuf.at[j, p]
    tree = gather_tree(wire, place.over_group, HOPS, nbuf.at[0, 0], slot_n, cut, False)
    sum_g = SumTree(
        wire, place.over_group, HOPS, lambda j, p: part_g.at[j, p], cut,
        [g_half.at[k] for k in range(14)],
    )

    def cut_d(ref, part):
        start, size = ((0, 1152), (0, 640), (640, 512))[part]
        return ref.at[:, pl.ds(start, size)]

    quarter_d = dd.at[core, y]
    swap_d = wire.copy(dd.at[1 - core], r_d, sibling)
    sum_d = SumTree(
        wire, lambda dx, mirror: place.device(dy=dx), RING,
        lambda j, p: dd.at[core, (y + STEPS[j]) % 4], cut_d,
        [d_whole.at[0], d_whole.at[1], d_half_a, d_half_b],
    )
    cross_d = wire.copy(quarter_d, z_d, low)

    def cut_lead(ref, part):
        return ref if part == 0 else ref.at[pl.ds((part - 1) * 4, 4)]

    swap_gu = wire.copy(dgu.at[1 - core], r_gu, sibling)
    far_b = SumTree(
        wire, place.over_group, HOPS_FAR, lambda j, p: part_b.at[j, p], cut,
        [b_half.at[k] for k in range(4)],
    )
    far_gu = [
        wire.copy(
            cut_lead(dgu.at[core, (y + 2) % 4], part),
            gu_half.at[part - 1],
            place.device(dy=(3, 1)[part - 1]),
        )
        for part in (1, 2)
    ]
    loads[0].wait()
    for k in FIRST:
        tree[k].start()
    wd[FF_DEV:] = jnp.zeros((FF_PAD - FF_DEV, wd.shape[1]), wd.dtype)
    loads[1].wait()
    loads[2].wait()

    def back_hidden(j):
        rows = jnp.concatenate([gb[j, 0], gb[j, 1]], axis=0)
        gh[j] = trail_product(rows, wd[...])

    def forward(j):
        rows = jnp.concatenate([nbuf[j, 0], nbuf[j, 1]], axis=0)

        def tile(t, carry):
            columns = pl.ds(pl.multiple_of(t * 256, 256), 256)
            narrow = pl.ds(pl.multiple_of(t * 128, 128), 128)
            both = matmul(rows, wgu[:, columns])
            gate, up = both[:, :128], both[:, 128:]
            square = gate * gate
            curve = jnp.tanh(ROOT * gate * (1.0 + CUBE * square))
            half_up = 0.5 * (1.0 + curve)
            active = gate * half_up
            slope = half_up + 0.5 * gate * (1.0 - curve * curve) * (
                ROOT * (1.0 + 3.0 * CUBE * square)
            )
            back = gh[j, :, narrow]
            hid[j, :, narrow] = (active * up).astype(jnp.bfloat16)
            ggu[j, :, columns] = jnp.concatenate(
                [(back * up * slope).astype(jnp.bfloat16), (back * active).astype(jnp.bfloat16)],
                axis=1,
            )
            return carry

        lax.fori_loop(0, PAIRS, tile, 0)

    def back_normed(j):
        for start, size in ((0, 512), (512, 512), (1024, 128)):
            block = trail_product(ggu[j], wgu[start : start + size, :]).astype(jnp.bfloat16)
            part_g[j, 0, :, start : start + size] = block[:192]
            part_g[j, 1, :, start : start + size] = block[192:]

    def down(j):
        for start, size in ((0, 512), (512, 512), (1024, 128)):
            block = matmul(hid[j], wd[:, start : start + size]).astype(jnp.bfloat16)
            part_b[j, 0, :, start : start + size] = block[:192]
            part_b[j, 1, :, start : start + size] = block[192:]

    hid_rows = hid.reshape(4 * 384, FF_PAD)
    ggu_rows = ggu.reshape(4 * 384, 2 * FF_PAD)
    gb_rows = gb.reshape(4 * 384, 1152)
    dd_rows = dd.reshape(FF_PAD, 1152)
    dgu_rows = dgu.reshape(2, 4, 1152, 256)

    def turn_rows(j):
        rows = jnp.concatenate([nbuf[j, 0], nbuf[j, 1]], axis=0)
        n_turned[:, 384 * j : 384 * (j + 1)] = rows.T

    def grad_half(half):
        def tile(q, carry):
            columns = pl.ds(pl.multiple_of((half * 4 + q) * 256, 256), 256)
            dgu_rows[half, q] = matmul(n_turned[...], ggu_rows[:, columns]).astype(jnp.bfloat16)
            return carry

        lax.fori_loop(0, 3, tile, 0)

    dgu[:, 3, :, :, 128:] = jnp.zeros((2, 8, 144, 128), jnp.bfloat16)
    back_hidden(0)
    back_hidden(1)
    back_hidden(2)
    for k in SERVE[:3]:
        arrive(tree, k)
    back_hidden(3)
    for k in SERVE[3:7]:
        arrive(tree, k)
    loads[3].wait()
    forward(0)
    turn_rows(0)
    for k in SERVE[7:9]:
        arrive(tree, k)
    forward(1)
    for k in SERVE[9:12]:
        arrive(tree, k)
    forward(2)
    turn_rows(1)
    turn_rows(2)
    for k in SERVE[12:]:
        arrive(tree, k)
    forward(3)
    back_normed(3)
    sum_g.send_far()
    back_normed(1)
    back_normed(2)
    sum_g.send_mid()
    for start, size in ((0, 512), (512, 512), (1024, 128)):
        dd_rows[:, start : start + size] = lead_product(
            hid_rows[...], gb_rows[:, start : start + size]
        ).astype(jnp.bfloat16)
    swap_d.start()
    sum_g.send_near()
    back_normed(0)
    sum_g.start(1)
    turn_rows(3)
    middle_tile = matmul(n_turned[...], ggu_rows[:, 768:1024]).astype(jnp.bfloat16)
    dgu_rows[0, 3, :, :128] = middle_tile[:, :128]
    dgu_rows[1, 3, :, :128] = middle_tile[:, 128:]
    down(3)
    swap_d.wait_recv()

    def add_d(i, carry):
        add_into(dd.at[core, i], r_d.at[i])
        return carry

    lax.fori_loop(0, 4, add_d, 0)
    sum_d.start(2, 3)
    sum_g.send_next()
    grad_half(1 - core)
    swap_gu.start()
    sum_g.send_last()
    far_b.start(0, 1, 2, 3)
    sum_d.absorb(2, 3)
    sum_d.start(0, 1)
    grad_half(core)
    down(0)
    swap_gu.wait_recv()

    def add_gu(i, carry):
        add_into(dgu.reshape(2, 32, 144, 256).at[core, i], r_gu.reshape(32, 144, 256).at[i])
        return carry

    lax.fori_loop(0, 32, add_gu, 0)
    for copy in far_gu:
        copy.start()
    sum_d.absorb(0, 1)
    cross_d.start()
    down(1)
    down(2)
    out_f32[...] = sum_g.finish(0)
    store_g = pltpu.make_async_copy(out_f32, o_gn, local_sems.at[6])
    store_g.start()
    cross_d.wait_recv()
    cross_d.wait_send()
    add_into(quarter_d, z_d)
    store_d = pltpu.make_async_copy(quarter_d, o_pd, local_sems.at[7])
    store_d.start()
    far_b.absorb(0, 1, 2, 3)
    store_b = pltpu.make_async_copy(part_b, o_pb, local_sems.at[5])
    store_b.start()
    for part, j in ((1, 2), (2, 1)):
        far_gu[part - 1].wait_recv()
        add_into(
            cut_lead(dgu.at[core, (y + STEPS[j]) % 4], part), gu_half.at[part - 1]
        )
    store_gu = pltpu.make_async_copy(dgu.at[core], o_pgu, local_sems.at[4])
    store_gu.start()
    for store in (store_b, store_gu, store_g, store_d):
        store.wait()
    for copy in wire.made:
        if copy is not cross_d:
            copy.wait_send()


def feed_forward(own_n, gb_all, wgu_all, wd_all):
    bf, f32 = jnp.bfloat16, jnp.float32
    vm = pltpu.VMEM
    tokens, width = own_n.shape
    sums = [vm((14, tokens // 2, width), bf)]
    return pl.pallas_call(
        ff_kernel,
        out_shape=(
            jax.ShapeDtypeStruct((tokens, width), f32),
            jax.ShapeDtypeStruct((4, 2, tokens, width), bf),
            jax.ShapeDtypeStruct((4, 8, 144, 256), bf),
            jax.ShapeDtypeStruct((112, width), bf),
        ),
        in_specs=[ANY] * 4,
        out_specs=(ANY,) * 4,
        scratch_shapes=[
            vm((4, 2, tokens, width), bf),
            vm((4, 2, tokens, width), bf),
            vm(wgu_all.shape, bf),
            vm((FF_PAD, width), bf),
            vm((4, 2 * tokens, FF_PAD), f32),
            vm((4, 2 * tokens, FF_PAD), bf),
            vm((4, 2 * tokens, 2 * FF_PAD), bf),
            vm((4, 2, tokens, width), bf),
            vm((4, 2, tokens, width), bf),
            vm((tokens, width), f32),
            vm((2, 4, 8, 144, 256), bf),
        ]
        + sums
        + [
            vm((2, 4, 112, width), bf),
            vm((4, 112, width), bf),
            vm((2, 112, width), bf),
            vm((112, 640), bf),
            vm((112, 512), bf),
            vm((112, width), bf),
            vm((4, 8, 144, 256), bf),
            vm((2, 4, 144, 256), bf),
            vm((width, 8 * tokens), bf),
            vm((4, tokens // 2, width), bf),
        ]
        + [
            pltpu.SemaphoreType.DMA((8,)),
            pltpu.SemaphoreType.DMA((48,)),
            pltpu.SemaphoreType.DMA((48,)),
        ],
        compiler_params=comm_params(2),
        name="feed_forward",
    )(own_n, gb_all, wgu_all, wd_all)


def back_kernel(
    p_gu, p_d, part_b_all, gn2_all, middle_all, miscs_all, tokens, cot, rope_all, q_all, kv_all,
    probs_all, att_all, wqkv_all, wo_all, normed1_all,
    o_gu, o_d, o_q, o_kv, o_wo, o_out, o_grad,
    h_gu, gu_whole, z_gu, f_gu, piece_d,
    part_b, b_half, gn2, middle, miscs, x_ref, cot_ref, rope, q_ref, kv_ref, probs, att,
    wqkv, wo, normed1, dq, r_q, q_half, dkv, r_kv, kv_parts, dwo, r_wo, w_half,
    gkv, kv_out, kv_in, gproj, gmid, out_bf,
    s_wo, y_wo, z_wo, s_q, y_q, z_q, s_kv, y_kv, z_kv,
    local_sems, send_sems, recv_sems,
):
    place = Place()
    wire = Wire(send_sems, recv_sems)
    core, me, y, rep = place.core, place.shard, place.y, place.rep
    rows, width = tokens.shape
    at = place.shard_at
    others = [(j, p) for p in (0, 1) for j in range(4) if (j, p) != (0, 0)]
    group = [place.device(dx=STEPS[j], mirror=p) for j, p in others]
    sequence = [(rep, at(j, 1)) for j in range(4)]
    sibling = place.device(sibling=1)
    column = [place.device(dy=d) for d in (1, 3, 2)]
    low = place.device(swap_lo=1)
    locals_ = []

    def local(src, dst):
        copy = pltpu.make_async_copy(src, dst, local_sems.at[len(locals_)])
        copy.start()
        locals_.append(copy)
        return copy

    loads = [
        local(src, dst)
        for src, dst in (
            (miscs_all, miscs),
            (gn2_all, gn2),
            (middle_all, middle),
            (cot, cot_ref),
            (att_all, att),
            (wo_all, wo),
        )
    ]
    load_gu = local(p_gu, h_gu)
    load_d = local(p_d, piece_d)
    load_b = local(part_b_all, part_b)
    both_cores = [place.device(dy=d, sibling=1) for d in (1, 3, 2)]
    greet([sibling, low] + group + column + sequence + both_cores)
    loads_heads = [
        local(src, dst)
        for src, dst in ((q_all, q_ref), (kv_all, kv_ref), (probs_all, probs), (rope_all, rope))
    ]
    load_x = local(tokens, x_ref)
    load_n = local(normed1_all, normed1)
    load_w = local(wqkv_all, wqkv)
    loaded = len(locals_)

    def over_y(dx, mirror):
        return place.device(dy=dx)

    def cut_lead(ref, part):
        return ref if part == 0 else ref.at[pl.ds((part - 1) * 4, 4)]

    def cut_rows(size):
        def cut(ref, part):
            return ref if part == 0 else ref.at[pl.ds((part - 1) * size, size)]

        return cut

    def cut_lanes(size):
        def cut(ref, part):
            return ref if part == 0 else ref.at[:, pl.ds((part - 1) * size, size)]

        return cut

    def cut_d(ref, part):
        start, size = ((0, width), (0, 640), (640, 512))[part]
        return ref.at[:, pl.ds(start, size)]

    def added(target, source, count):
        def one(i, carry):
            add_into(target.at[i], source.at[i])
            return carry

        lax.fori_loop(0, count, one, 0)

    chunks = [pl.ds(0, 80), pl.ds(80, 64)]
    near_gu = [
        [
            wire.copy(
                h_gu.at[(y + STEPS[j]) % 4, :, c],
                gu_whole.at[k, :, c],
                place.device(dy=(3, 1)[k]),
            )
            for k, j in enumerate((2, 1))
        ]
        for c in chunks
    ]
    quarters = [h_gu.at[y, :, c] for c in chunks]
    crossings_gu = [wire.copy(h_gu.at[y, :, c], z_gu.at[:, c], low) for c in chunks]
    turns = [
        [
            wire.copy(h_gu.at[y, at(j, p), c], f_gu.at[me, c], device)
            for (j, p), device in zip(others, group)
        ]
        for c in chunks
    ]
    slots_gu = [lambda j, p, c=c: o_gu.at[core, (y + STEPS[j]) % 4, :, c] for c in chunks]
    trees_gu = [
        gather_tree(wire, over_y, RING, f_gu.at[:, c], slot, cut_lead, True)
        for c, slot in zip(chunks, slots_gu)
    ]
    passes_gu = [
        [
            wire.copy(f_gu.at[:, c] if j == 0 else slot(j, 0), slot(j, 0), sibling)
            for j in range(4)
        ]
        for c, slot in zip(chunks, slots_gu)
    ]

    def cross(i):
        for k, copy in enumerate(near_gu[i]):
            copy.wait_recv()
            added(quarters[i], gu_whole.at[k, :, chunks[i]], 8)
        crossings_gu[i].start()

    def turn(i):
        crossings_gu[i].wait_recv()
        crossings_gu[i].wait_send()
        added(quarters[i], z_gu.at[:, chunks[i]], 8)
        for copy in turns[i]:
            copy.start()
        f_gu[me, chunks[i]] = h_gu[y, me, chunks[i]]

    def spread(i):
        for copy in turns[i]:
            copy.wait_recv()
        for copy in (trees_gu[i][0], trees_gu[i][1], passes_gu[i][0]):
            copy.start()
        local(f_gu.at[:, chunks[i]], slots_gu[i](0, 0))

    def spread_on(i, k):
        arrive(trees_gu[i], k, RING_ONWARD)
        if k != 2:
            passes_gu[i][(2, 1, None, 3)[k]].start()

    load_gu.wait()
    for copy in near_gu[0] + near_gu[1]:
        copy.start()

    sum_b = SumTree(
        wire, place.over_group, HOPS, lambda j, p: part_b.at[j, p], cut_rows(96),
        [b_half.at[k] for k in range(14)],
    )
    load_b.wait()
    sum_b.start(7, 6, 4, 2, 11, 10, 1)

    load_d.wait()
    slot_d = lambda j, p: o_d.at[core, (y + STEPS[j]) % 4]
    tree_d = gather_tree(wire, over_y, RING, piece_d, slot_d, cut_d, True)
    pass_d = [
        wire.copy(piece_d if j == 0 else slot_d(j, 0), slot_d(j, 0), sibling) for j in range(4)
    ]

    for load in loads:
        load.wait()
    as_float = [miscs[s].astype(jnp.float32) for s in range(8)]
    gain1 = jnp.concatenate([m[0:1, :144] for m in as_float], axis=1)
    gain2 = jnp.concatenate([m[1:2, :144] for m in as_float], axis=1)
    row = lax.broadcasted_iota(jnp.int32, (rows, 1), 0).astype(jnp.float32)
    keep = jnp.where(row < miscs[me].astype(jnp.float32)[2:3, :1], 1.0, 0.0)
    mid = middle[...]
    inverse2 = lax.rsqrt(jnp.mean(mid * mid, axis=1, keepdims=True) + EPSILON)
    scaled2 = mid * inverse2
    grad2 = gn2[...]
    grad_gain2 = jnp.sum(grad2 * scaled2, axis=0, keepdims=True)
    grad2 = grad2 * gain2
    grad_mid = cot_ref[...].astype(jnp.float32) + inverse2 * (
        grad2 - scaled2 * jnp.mean(grad2 * scaled2, axis=1, keepdims=True)
    )
    gmid[...] = grad_mid
    grad_attn = (keep * grad_mid).astype(jnp.bfloat16)
    for start in range(0, width, 384):
        block = lead_product(att[...], grad_attn[:, start : start + 384]).astype(jnp.bfloat16)
        block = block.reshape(8, 2, 64, 384)
        dwo[0, :, :, start : start + 384] = block[:, 0]
        dwo[1, :, :, start : start + 384] = block[:, 1]
    swap_wo = wire.copy(dwo.at[1 - core], r_wo, sibling)
    swap_wo.start()
    grad_att = trail_product(grad_attn, wo.reshape(1024, width)[...]).astype(jnp.bfloat16)

    for load in loads_heads:
        load.wait()
    keys = (BEHIND + 1) * rows
    all_kv = kv_ref.reshape(keys, 512)
    flat = gkv.reshape(keys, 512)
    cosine, sine_part = rope[:, :128], rope[:, 128:]
    scaling = 256 ** (-0.5)

    def turned_back(vectors):
        first, second = vectors[:, :128], vectors[:, 128:]
        return jnp.concatenate(
            [first * cosine + second * sine_part, second * cosine - first * sine_part], axis=1
        )

    for h in range(4):
        share = probs[h]
        share_low = share.astype(jnp.bfloat16)
        grad_h = grad_att[:, 256 * h : 256 * (h + 1)]
        grad_probs = trail_product(grad_h, all_kv[:, 256:])
        delta = jnp.sum(share * grad_probs, axis=1, keepdims=True)
        grad_scores = (share * (grad_probs - delta)).astype(jnp.bfloat16)
        grad_keys = lead_product(grad_scores, q_ref[h])
        grad_values = lead_product(share_low, grad_h)
        if h == 0:
            flat[:, :256] = grad_keys
            flat[:, 256:] = grad_values
        else:
            flat[:, :256] += grad_keys
            flat[:, 256:] += grad_values
        grad_q = matmul(grad_scores, all_kv[:, :256])
        gproj[:, 256 * h : 256 * (h + 1)] = (turned_back(grad_q) * scaling).astype(jnp.bfloat16)
        if h == 1:
            cross(0)
            for copy in (tree_d[0], tree_d[1], pass_d[0]):
                copy.start()
            local(piece_d, slot_d(0, 0))
    x, upper = place.x, place.z_hi == 1
    sends = []
    for i in range(1, BEHIND):
        kv_out[i - 1] = gkv[i].astype(jnp.bfloat16)
        target = (rep, 4 * place.z_hi + (x + (4 - i)) % 4)
        sends.append(wire.copy(kv_out.at[i - 1], kv_in.at[i - 1], target))
        pl.when(jnp.logical_or(upper, x >= i))(sends[-1].start)

        @pl.when(jnp.logical_not(jnp.logical_or(upper, x + i <= 3)))
        def _():
            kv_in[i - 1] = jnp.zeros(kv_in.shape[1:], kv_in.dtype)

    plane_kv = wire.copy(kv_out.at[BEHIND - 1], kv_in.at[BEHIND - 1], (rep, at(0, 1)))

    @pl.when(upper)
    def _():
        kv_in[BEHIND - 1] = jnp.zeros(kv_in.shape[1:], kv_in.dtype)

    def collect_kv():
        through = gkv[BEHIND]
        for i, copy in enumerate(sends):
            pl.when(jnp.logical_or(upper, x + (i + 1) <= 3))(copy.wait_recv)
            through = through + jnp.where(x + (i + 1) > 3, 1.0, 0.0) * kv_in[i].astype(jnp.float32)
        kv_out[BEHIND - 1] = through.astype(jnp.bfloat16)
        pl.when(upper)(plane_kv.start)

    load_n.wait()
    dq_rows = dq.reshape(2, width, 512)
    for t in range(4):
        dq_rows[t // 2, :, 256 * (t % 2) : 256 * (t % 2 + 1)] = lead_product(
            normed1[...], gproj[:, 256 * t : 256 * (t + 1)]
        ).astype(jnp.bfloat16)
    swap_q = wire.copy(dq.at[1 - core], r_q, sibling)
    swap_q.start()
    swap_wo.wait_recv()
    added(dwo.at[core], r_wo, 8)
    sum_wo = SumTree(
        wire, place.over_group, HOPS, lambda j, p: dwo.at[core, at(j, p)], cut_rows(32),
        [w_half.at[k] for k in range(14)],
    )
    sum_wo.send_far()
    sum_wo.send_mid()
    sum_wo.start(1)
    cross(1)
    collect_kv()
    load_x.wait()
    load_w.wait()
    weights = wqkv.reshape(width, 1536)
    gn2[...] = trail_product(gproj[:, :1024], weights[:, :1024])
    swap_q.wait_recv()
    added(dq.at[core], r_q, 8)
    sum_q = SumTree(
        wire, place.over_group, HOPS, lambda j, p: dq.at[core, at(j, p)], cut_lanes(256),
        [q_half.at[k] for k in range(14)],
    )
    sum_q.send_far()
    sum_q.send_mid()
    sum_q.start(1)
    turn(0)

    pl.when(jnp.logical_not(upper))(plane_kv.wait_recv)
    grad_kv = gkv[0] + kv_in[BEHIND - 1].astype(jnp.float32)
    for i in range(BEHIND - 1):
        grad_kv = grad_kv + jnp.where(x + (i + 1) <= 3, 1.0, 0.0) * kv_in[i].astype(jnp.float32)
    gproj[:, 1024:1280] = turned_back(grad_kv[:, :256]).astype(jnp.bfloat16)
    gproj[:, 1280:1536] = grad_kv[:, 256:].astype(jnp.bfloat16)
    for t in range(2):
        dkv[t, :, :144] = (
            lead_product(normed1[...], gproj[:, 1024 + 256 * t : 1280 + 256 * t])
            .astype(jnp.bfloat16)
            .reshape(8, 144, 256)
        )
    inputs = x_ref[...].astype(jnp.float32)
    inverse1 = lax.rsqrt(jnp.mean(inputs * inputs, axis=1, keepdims=True) + EPSILON)
    scaled1 = inputs * inverse1
    grad1 = gn2[...] + trail_product(gproj[:, 1024:], weights[:, 1024:])
    grad_gain1 = jnp.sum(grad1 * scaled1, axis=0, keepdims=True)
    for s in range(8):
        cols = slice(144 * s, 144 * (s + 1))
        both = jnp.concatenate(
            [grad_gain1[:, cols], grad_gain2[:, cols], jnp.zeros((14, 144), jnp.float32)], axis=0
        )
        both = jnp.concatenate([both, jnp.zeros((16, 112), jnp.float32)], axis=1)
        dkv[0, s, 144:] = both.astype(jnp.bfloat16)
        dkv[1, s, 144:] = both.astype(jnp.bfloat16)
    swap_kv = wire.copy(dkv.at[1 - core], r_kv, sibling)
    swap_kv.start()
    turn(1)
    sum_wo.send_near()
    swap_kv.wait_recv()
    added(dkv.at[core], r_kv, 8)
    direct_kv = [
        wire.copy(dkv.at[core, at(j, p)], kv_parts.at[i], device)
        for i, ((j, p), device) in enumerate(zip(others, group))
    ]
    for copy in direct_kv:
        copy.start()
    spread(0)
    grad1 = grad1 * gain1
    gmid[...] += inverse1 * (grad1 - scaled1 * jnp.mean(grad1 * scaled1, axis=1, keepdims=True))
    local(gmid, o_grad)
    for k in (0, 1):
        arrive(tree_d, k, RING_ONWARD)
        pass_d[(2, 1)[k]].start()
    spread(1)
    sum_q.send_near()
    sum_wo.send_next()
    sum_wo.send_last()
    sum_q.send_next()
    sum_q.send_last()
    for k in (0, 1):
        spread_on(0, k)
    sum_b.absorb(10)
    sum_b.start(3)
    sum_b.absorb(11)
    sum_b.start(5)
    sum_b.send_last()

    def over_column(source, landing):
        copies = [
            wire.copy(source.at[(y + d) % 4], landing.at[i], device)
            for i, (d, device) in enumerate(zip((1, 3, 2), column))
        ]
        for copy in copies:
            copy.start()
        return copies

    def over_low(copies, source, landing, other):
        for copy in copies:
            copy.wait_recv()
        mine = source[y].astype(jnp.float32)
        for i in range(3):
            mine = mine + landing[i].astype(jnp.float32)
        source[y] = mine.astype(jnp.bfloat16)
        crossing = wire.copy(source.at[y], other, low)
        crossing.start()
        return crossing

    def to_all(crossing, source, other, slot):
        crossing.wait_recv()
        crossing.wait_send()
        add_into(source.at[y], other)
        made = [wire.copy(source.at[y], slot(core, y), device) for device in column + [sibling]]
        for copy in made:
            copy.start()
        local(source.at[y], slot(core, y))
        return made

    def to_both(crossing, source, other, slot):
        made = to_all(crossing, source, other, slot)
        made += [
            wire.copy(source.at[y], slot(core, y), place.device(dy=d, sibling=1)) for d in (1, 3, 2)
        ]
        for copy in made[4:]:
            copy.start()
        return made

    def pass_on(made, slot):
        ends = [made[3]]
        for d, copy in zip((3, 1, 2), made):
            copy.wait_recv()
            held = slot(core, (y + d) % 4)
            ends.append(wire.copy(held, held, sibling))
            ends[-1].start()
        return ends

    slot_wo = lambda c, q: o_wo.at[c, q]
    slot_q = lambda c, q: o_q.at[:, pl.ds(pl.multiple_of(c * 512 + q * 128, 128), 128)]
    slot_kv = lambda c, q: o_kv.at[c, q]
    s_wo[...] = sum_wo.finish(0).astype(jnp.bfloat16).reshape(4, 16, width)
    over_wo = over_column(s_wo, y_wo)
    total = sum_q.finish(1).astype(jnp.bfloat16)
    for q in range(4):
        s_q[q] = total[:, 128 * q : 128 * (q + 1)]
    over_q = over_column(s_q, y_q)
    for k in (0, 1):
        spread_on(1, k)
    cross_wo = over_low(over_wo, s_wo, y_wo, z_wo)
    cross_q = over_low(over_q, s_q, y_q, z_q)
    total = dkv[core, me].astype(jnp.float32)
    for i, copy in enumerate(direct_kv):
        copy.wait_recv()
        total = total + kv_parts[i].astype(jnp.float32)
    s_kv[0] = total[:144, :128].astype(jnp.bfloat16)
    s_kv[1] = total[:144, 128:].astype(jnp.bfloat16)
    s_kv[2] = jnp.concatenate(
        [total[144:, :128], total[144:, 128:], jnp.zeros((112, 128), jnp.float32)], axis=0
    ).astype(jnp.bfloat16)
    s_kv[3] = jnp.zeros((144, 128), jnp.bfloat16)
    over_kv = over_column(s_kv, y_kv)
    for k in (2, 3):
        arrive(tree_d, k, RING_ONWARD)
    pass_d[3].start()
    all_wo = to_all(cross_wo, s_wo, z_wo, slot_wo)
    all_q = to_all(cross_q, s_q, z_q, slot_q)
    cross_kv = over_low(over_kv, s_kv, y_kv, z_kv)
    for k in (2, 3):
        spread_on(0, k)
    all_kv_sum = to_both(cross_kv, s_kv, z_kv, slot_kv)
    ends = pass_on(all_wo, slot_wo) + pass_on(all_q, slot_q)
    for k in (2, 3):
        spread_on(1, k)
    out_bf[...] = (middle[...] + keep * sum_b.finish(0)).astype(jnp.bfloat16)
    local(out_bf, o_out)
    ends += all_kv_sum
    for copy in pass_d + passes_gu[0] + passes_gu[1] + ends:
        copy.wait_recv()
    for copy in locals_[loaded:]:
        copy.wait()
    for i, copy in enumerate(sends):
        pl.when(jnp.logical_or(upper, x >= i + 1))(copy.wait_send)
    pl.when(upper)(plane_kv.wait_send)
    waited = [id(copy) for copy in sends + [plane_kv] + crossings_gu + [cross_wo, cross_q, cross_kv]]
    waited += [id(sum_b.copies[k]) for k in (8, 9, 12, 13)]
    for copy in wire.made:
        if id(copy) not in waited:
            copy.wait_send()


def back(*args):
    bf, f32 = jnp.bfloat16, jnp.float32
    width = 1152
    rows = args[6].shape[0]
    outs = [
        ((2, 4, 8, 144, 256), bf),
        ((2, 4, 112, width), bf),
        ((144, 1024), bf),
        ((2, 4, 144, 128), bf),
        ((2, 4, 16, width), bf),
        ((rows, width), bf),
        ((rows, width), f32),
    ]
    scratch = [
        ((4, 8, 144, 256), bf),
        ((2, 8, 144, 256), bf),
        ((8, 144, 256), bf),
        ((8, 144, 256), bf),
        ((112, width), bf),
        ((4, 2, rows, width), bf),
        ((14, rows // 2, width), bf),
    ]
    scratch += [(a.shape, a.dtype) for a in args[3:16]]
    for whole, parts in (
        ((144, 512), (14, 144, 256)),
        ((160, 256), (7, 160, 256)),
        ((64, width), (14, 32, width)),
    ):
        scratch += [((2, 8, *whole), bf), ((8, *whole), bf), (parts, bf)]
    scratch += [
        ((BEHIND + 1, rows, 512), f32),
        ((BEHIND, rows, 512), bf),
        ((BEHIND, rows, 512), bf),
        ((rows, 1536), bf),
        ((rows, width), f32),
        ((rows, width), bf),
    ]
    for piece in ((16, width), (144, 128), (144, 128)):
        scratch += [((4, *piece), bf), ((3, *piece), bf), (piece, bf)]
    return pl.pallas_call(
        back_kernel,
        out_shape=tuple(jax.ShapeDtypeStruct(*o) for o in outs),
        in_specs=[ANY] * 16,
        out_specs=(ANY,) * len(outs),
        scratch_shapes=[pltpu.VMEM(*v) for v in scratch]
        + [
            pltpu.SemaphoreType.DMA((40,)),
            pltpu.SemaphoreType.DMA((176,)),
            pltpu.SemaphoreType.DMA((176,)),
        ],
        compiler_params=comm_params(3),
        name="attention_backward",
    )(*args)


def on_device(
    tokens, lengths, attn_gain, w_query, w_keyval, w_out, mlp_gain, w_gate, w_up, w_down, cotangent
):
    width = tokens.shape[1]
    live_count = lengths[0, 0]
    row = lax.broadcasted_iota(jnp.int32, (16, 256), 0)
    wide = lambda gain: jnp.pad(gain, (0, 112))[None]
    misc = jnp.where(
        row == 0,
        wide(attn_gain),
        jnp.where(row == 1, wide(mlp_gain), live_count.astype(jnp.bfloat16)),
    )
    frequency = np.power(10000.0, -2.0 * np.arange(128) / 256).astype(np.float32)
    (
        miscs, qkv_all, out_all, gu_all, branch_all,
        normed1, queries, all_kv, probs, attended, middle, normed2, rope,
    ) = front(
        tokens, cotangent, misc, jnp.asarray(np.tile(frequency[None], (8, 1))),
        w_query, w_keyval, w_out, w_gate, w_up,
    )
    grad_normed2, branch, grad_gu, grad_d = feed_forward(
        normed2, branch_all, gu_all.reshape(width, -1), w_down
    )
    sum_gu, sum_d, sum_q, sum_kv, sum_wo, outputs, grad_inputs = back(
        grad_gu, grad_d, branch, grad_normed2, middle, miscs, tokens, cotangent,
        rope, queries, all_kv, probs, attended, qkv_all, out_all, normed1,
    )
    grad_gate_w, grad_up_w, grad_down, grad_q, grad_kv, grad_wo = finish(
        sum_gu, sum_d.reshape(FF_PAD, width), sum_q, sum_kv, sum_wo.reshape(128, width)
    )
    gains = sum_kv[0, 2]
    gains = jnp.concatenate([gains[:2], gains[16:18, :16]], axis=1).astype(jnp.float32)
    return (
        outputs,
        grad_inputs,
        gains[0],
        grad_q,
        grad_kv,
        grad_wo,
        gains[1],
        grad_gate_w,
        grad_up_w,
        grad_down,
    )


def solution(mesh):
    placed = (
        P(("rep", "shard"), None),
        P("rep", "shard"),
        P("shard"),
        P("shard", None),
        P("shard", None),
        P("shard", None),
        P("shard"),
        P("shard", None),
        P("shard", None),
        P("shard", None),
        P(("rep", "shard"), None),
    )
    return jax.shard_map(
        on_device,
        mesh=mesh,
        in_specs=placed,
        out_specs=(
            P(("rep", "shard"), None),
            P(("rep", "shard"), None),
            P("shard"),
            P("shard", None),
            P("shard", None),
            P("shard", None),
            P("shard"),
            P("shard", None),
            P("shard", None),
            P("shard", None),
        ),
        check_vma=False,
    )
```

profile of v0, /device:TPU:1, one launch (start us, length us, event | category | flops | bytes accessed | tf_op | source)
XLA Modules:
  0.0 256.7 jit_solution(3590347519564860182)
XLA Ops:
  1.3 0.7 pad.7
  2.0 0.7 pad.8
  2.6 0.7 select_select_fusion.misc
  3.3 64.2 %attention_forward.1 = (bf16[8,16,256]{2,1,0:T(8,128)(2,1)}, bf16[8,144,1536]{2,1,0:T(8,128)(2,1)}, bf16[8,128,1152]{2,1,0:T(8,128)(2,1)}, bf16[8,144,1792]{2,1,...) custom-call(bf16[192,1152]{1,0:T(8,128)(2,1)} %tokens.3, ...), custom_call_target="tpu_custom_call" | custom-call | tf_op jit(solution)/shard_map/attention_forward/pallas_call | solution.py:558
  67.5 86.5 %feed_forward.1 = (f32[192,1152]{1,0:T(8,128)}, bf16[4,2,192,1152]{3,2,1,0:T(8,128)(2,1)}, bf16[4,8,144,256]{3,2,1,0:T(8,128)(2,1)}, bf16[112,1152]{1,0:T(8,128)(2,1)}) custom-call(bf16[192,1152]{1,0:T(8,128)(2,1)} %get-tuple-element.40.own_n, bf16[4,2,192,1152]{3,2,1,0:T(8,128)(2,1)} %get-tuple-element.41.gb_all, bf16[1152,1792]{1,0:T(8,128)(2,1)} %bitcast.10, ...), custom_call_target="tpu_custom_call" | custom-call | tf_op jit(solution)/shard_map/feed_forward/pallas_call | solution.py:854
  154.0 88.2 %attention_backward.1 = (bf16[2,4,8,144,256]{4,3,2,1,0:T(8,128)(2,1)}, bf16[2,4,112,1152]{3,2,1,0:T(8,128)(2,1)}, bf16[144,1024]{1,0:T(8,128)(2,1)}, bf16[2,4,14...) custom-call(bf16[4,8,144,256]{3,2,1,0:T(8,128)(2,1)} %get-tuple-eleme, ...), custom_call_target="tpu_custom_call" | custom-call | tf_op jit(solution)/shard_map/attention_backward/pallas_call | solution.py:1383
  242.2 0.7 slice_bitcast_fusion.1
  242.9 0.8 slice_bitcast_fusion
  243.6 0.6 fusion
  244.2 0.0 copy-start.1
  244.2 0.0 copy-start
  244.2 10.6 %finish.1 = (f32[144,6912]{1,0:T(8,128)}, f32[144,6912]{1,0:T(8,128)}, f32[864,1152]{1,0:T(8,128)}, f32[144,1024]{1,0:T(8,128)}, f32[144,512]{1,0:T(8,128)}, /*index=5*/f32[128,1152]{1,0:T(8,128)}) custom-call(bf16[2,4,8,144,256]{4,3,2,1,0:T(8,128)(2,1)} %get-tuple-element.60.both, bf16[896,1152]{1,0:T(8,128)(2,1)} %bitcast.11, ...), custom_call_target="tpu_custom_call" | custom-call | tf_op jit(solution)/shard_map/finish/pallas_call | solution.py:602
  254.9 0.0 copy-done.1
  254.9 0.8 copy.25
  255.6 0.0 copy-done
  255.6 0.9 copy.26
  (3 shorter events, 0.0 us)
Async XLA Ops:
  244.2 10.6 %copy-start.1 = (bf16[192,1152]{1,0:T(8,128)(2,1)S(1)}, bf16[192,1152]{1,0:T(8,128)(2,1)}, u32[]{:S(2)}) copy-start(bf16[192,1152]{1,0:T(8,128)(2,1)} %get-tuple-element.84) | copy-start | bytes 1327108
  244.2 11.4 %copy-start = (f32[192,1152]{1,0:T(8,128)S(1)}, f32[192,1152]{1,0:T(8,128)}, u32[]{:S(2)}) copy-start(f32[192,1152]{1,0:T(8,128)} %get-tuple-element.85) | copy-start | bytes 2654212
where the time goes:
time: 260 us; the launch traced here: 257 us
  Pallas kernels  249 us (96%)
  local copies, waits for them, and re-layouts  5.03 us (2%)
    pallas_call x1, Pallas kernels, back(): pl.pallas_call(back_kernel, out_shape=tuple((jax.ShapeDtypeStruct(*o) for...  88.2 us
    pallas_call x1, Pallas kernels, feed_forward(): pl.pallas_call(ff_kernel, out_shape=(jax.ShapeDtypeStruct((tokens, width)...  86.5 us
    pallas_call x1, Pallas kernels, front(): pl.pallas_call(front_kernel, out_shape=tuple((jax.ShapeDtypeStruct(*o) fo...  64.2 us
    pallas_call x1, Pallas kernels, finish(): pl.pallas_call(finish_kernel, grid=(steps,), out_shape=[jax.ShapeDtypeStr...  10.6 us

commit v1 on v0

--- a/solution.py
+++ b/solution.py
@@ -695,8 +695,10 @@
         rows = jnp.concatenate([gb[j, 0], gb[j, 1]], axis=0)
         gh[j] = trail_product(rows, wd[...])
 
-    def forward(j):
-        rows = jnp.concatenate([nbuf[j, 0], nbuf[j, 1]], axis=0)
+    def forward(j, first=0, count=384):
+        blocks = [nbuf[j, p] for p in (0, 1) if first <= 192 * p < first + count]
+        rows = jnp.concatenate(blocks, axis=0) if len(blocks) > 1 else blocks[0]
+        span = pl.ds(first, count)
 
         def tile(t, carry):
             columns = pl.ds(pl.multiple_of(t * 256, 256), 256)
@@ -704,27 +706,29 @@
             both = matmul(rows, wgu[:, columns])
             gate, up = both[:, :128], both[:, 128:]
             square = gate * gate
-            curve = jnp.tanh(ROOT * gate * (1.0 + CUBE * square))
-            half_up = 0.5 * (1.0 + curve)
+            curve = jnp.tanh(gate * (ROOT + ROOT * CUBE * square))
+            half_up = 0.5 + 0.5 * curve
             active = gate * half_up
-            slope = half_up + 0.5 * gate * (1.0 - curve * curve) * (
-                ROOT * (1.0 + 3.0 * CUBE * square)
-            )
-            back = gh[j, :, narrow]
-            hid[j, :, narrow] = (active * up).astype(jnp.bfloat16)
-            ggu[j, :, columns] = jnp.concatenate(
+            slope = half_up + active * (1.0 - curve) * (ROOT + 3.0 * ROOT * CUBE * square)
+            back = gh[j, span, narrow]
+            hid[j, span, narrow] = (active * up).astype(jnp.bfloat16)
+            ggu[j, span, columns] = jnp.concatenate(
                 [(back * up * slope).astype(jnp.bfloat16), (back * active).astype(jnp.bfloat16)],
                 axis=1,
             )
             return carry
 
-        lax.fori_loop(0, PAIRS, tile, 0)
-
-    def back_normed(j):
+        lax.fori_loop(0, PAIRS, tile, 0, unroll=True)
+
+    def back_normed(j, first=0, count=384):
         for start, size in ((0, 512), (512, 512), (1024, 128)):
-            block = trail_product(ggu[j], wgu[start : start + size, :]).astype(jnp.bfloat16)
-            part_g[j, 0, :, start : start + size] = block[:192]
-            part_g[j, 1, :, start : start + size] = block[192:]
+            block = trail_product(
+                ggu[j, first : first + count], wgu[start : start + size, :]
+            ).astype(jnp.bfloat16)
+            for p in (0, 1):
+                if first <= 192 * p < first + count:
+                    low = 192 * p - first
+                    part_g[j, p, :, start : start + size] = block[low : low + 192]
 
     def down(j):
         for start, size in ((0, 512), (512, 512), (1024, 128)):
@@ -770,11 +774,14 @@
     forward(2)
     turn_rows(1)
     turn_rows(2)
+    forward(3, 0, 192)
+    back_normed(3, 0, 192)
+    sum_g.start(9, 8)
     for k in SERVE[12:]:
         arrive(tree, k)
-    forward(3)
-    back_normed(3)
-    sum_g.send_far()
+    forward(3, 192, 192)
+    back_normed(3, 192, 192)
+    sum_g.start(13, 12)
     back_normed(1)
     back_normed(2)
     sum_g.send_mid()
@@ -903,7 +910,7 @@
     o_gu, o_d, o_q, o_kv, o_wo, o_out, o_grad,
     h_gu, gu_whole, z_gu, f_gu, piece_d,
     part_b, b_half, gn2, middle, miscs, x_ref, cot_ref, rope, q_ref, kv_ref, probs, att,
-    wqkv, wo, normed1, dq, r_q, q_half, dkv, r_kv, kv_parts, dwo, r_wo, w_half,
+    wqkv, wo, normed1, dq, r_q, q_parts, dkv, r_kv, kv_parts, dwo, r_wo, w_half,
     gkv, kv_out, kv_in, gproj, gmid, out_bf,
     s_wo, y_wo, z_wo, s_q, y_q, z_q, s_kv, y_kv, z_kv,
     local_sems, send_sems, recv_sems,
@@ -1156,6 +1163,7 @@
         ).astype(jnp.bfloat16)
     swap_q = wire.copy(dq.at[1 - core], r_q, sibling)
     swap_q.start()
+    cross(1)
     swap_wo.wait_recv()
     added(dwo.at[core], r_wo, 8)
     sum_wo = SumTree(
@@ -1165,22 +1173,23 @@
     sum_wo.send_far()
     sum_wo.send_mid()
     sum_wo.start(1)
-    cross(1)
-    collect_kv()
     load_x.wait()
     load_w.wait()
     weights = wqkv.reshape(width, 1536)
     gn2[...] = trail_product(gproj[:, :1024], weights[:, :1024])
+    turn(0)
     swap_q.wait_recv()
     added(dq.at[core], r_q, 8)
-    sum_q = SumTree(
-        wire, place.over_group, HOPS, lambda j, p: dq.at[core, at(j, p)], cut_lanes(256),
-        [q_half.at[k] for k in range(14)],
-    )
-    sum_q.send_far()
-    sum_q.send_mid()
-    sum_q.start(1)
-    turn(0)
+    direct_q = [
+        wire.copy(dq.at[core, at(j, p)], q_parts.at[i], device)
+        for i, ((j, p), device) in enumerate(zip(others, group))
+    ]
+    for copy in direct_q:
+        copy.start()
+    collect_kv()
+    turn(1)
+    sum_wo.send_near()
+    spread(0)
 
     pl.when(jnp.logical_not(upper))(plane_kv.wait_recv)
     grad_kv = gkv[0] + kv_in[BEHIND - 1].astype(jnp.float32)
@@ -1209,37 +1218,8 @@
         dkv[1, s, 144:] = both.astype(jnp.bfloat16)
     swap_kv = wire.copy(dkv.at[1 - core], r_kv, sibling)
     swap_kv.start()
-    turn(1)
-    sum_wo.send_near()
-    swap_kv.wait_recv()
-    added(dkv.at[core], r_kv, 8)
-    direct_kv = [
-        wire.copy(dkv.at[core, at(j, p)], kv_parts.at[i], device)
-        for i, ((j, p), device) in enumerate(zip(others, group))
-    ]
-    for copy in direct_kv:
-        copy.start()
-    spread(0)
-    grad1 = grad1 * gain1
-    gmid[...] += inverse1 * (grad1 - scaled1 * jnp.mean(grad1 * scaled1, axis=1, keepdims=True))
-    local(gmid, o_grad)
-    for k in (0, 1):
-        arrive(tree_d, k, RING_ONWARD)
-        pass_d[(2, 1)[k]].start()
     spread(1)
-    sum_q.send_near()
     sum_wo.send_next()
-    sum_wo.send_last()
-    sum_q.send_next()
-    sum_q.send_last()
-    for k in (0, 1):
-        spread_on(0, k)
-    sum_b.absorb(10)
-    sum_b.start(3)
-    sum_b.absorb(11)
-    sum_b.start(5)
-    sum_b.send_last()
-
     def over_column(source, landing):
         copies = [
             wire.copy(source.at[(y + d) % 4], landing.at[i], device)
@@ -1291,16 +1271,39 @@
     slot_wo = lambda c, q: o_wo.at[c, q]
     slot_q = lambda c, q: o_q.at[:, pl.ds(pl.multiple_of(c * 512 + q * 128, 128), 128)]
     slot_kv = lambda c, q: o_kv.at[c, q]
+    swap_kv.wait_recv()
+    added(dkv.at[core], r_kv, 8)
+    direct_kv = [
+        wire.copy(dkv.at[core, at(j, p)], kv_parts.at[i], device)
+        for i, ((j, p), device) in enumerate(zip(others, group))
+    ]
+    for copy in direct_kv:
+        copy.start()
+    sum_wo.send_last()
+    grad1 = grad1 * gain1
+    gmid[...] += inverse1 * (grad1 - scaled1 * jnp.mean(grad1 * scaled1, axis=1, keepdims=True))
+    local(gmid, o_grad)
+    total = dq[core, me].astype(jnp.float32)
+    for i, copy in enumerate(direct_q):
+        copy.wait_recv()
+        total = total + q_parts[i].astype(jnp.float32)
+    for q in range(4):
+        s_q[q] = total[:, 128 * q : 128 * (q + 1)].astype(jnp.bfloat16)
+    over_q = over_column(s_q, y_q)
+    for k in (0, 1):
+        arrive(tree_d, k, RING_ONWARD)
+        pass_d[(2, 1)[k]].start()
     s_wo[...] = sum_wo.finish(0).astype(jnp.bfloat16).reshape(4, 16, width)
     over_wo = over_column(s_wo, y_wo)
-    total = sum_q.finish(1).astype(jnp.bfloat16)
-    for q in range(4):
-        s_q[q] = total[:, 128 * q : 128 * (q + 1)]
-    over_q = over_column(s_q, y_q)
     for k in (0, 1):
-        spread_on(1, k)
+        spread_on(0, k)
+    cross_q = over_low(over_q, s_q, y_q, z_q)
+    sum_b.absorb(10)
+    sum_b.start(3)
+    sum_b.absorb(11)
+    sum_b.start(5)
+    sum_b.send_last()
     cross_wo = over_low(over_wo, s_wo, y_wo, z_wo)
-    cross_q = over_low(over_q, s_q, y_q, z_q)
     total = dkv[core, me].astype(jnp.float32)
     for i, copy in enumerate(direct_kv):
         copy.wait_recv()
@@ -1312,18 +1315,19 @@
     ).astype(jnp.bfloat16)
     s_kv[3] = jnp.zeros((144, 128), jnp.bfloat16)
     over_kv = over_column(s_kv, y_kv)
+    all_q = to_all(cross_q, s_q, z_q, slot_q)
+    all_wo = to_all(cross_wo, s_wo, z_wo, slot_wo)
+    for k in (0, 1):
+        spread_on(1, k)
+    cross_kv = over_low(over_kv, s_kv, y_kv, z_kv)
     for k in (2, 3):
         arrive(tree_d, k, RING_ONWARD)
     pass_d[3].start()
-    all_wo = to_all(cross_wo, s_wo, z_wo, slot_wo)
-    all_q = to_all(cross_q, s_q, z_q, slot_q)
-    cross_kv = over_low(over_kv, s_kv, y_kv, z_kv)
-    for k in (2, 3):
-        spread_on(0, k)
+    ends = pass_on(all_q, slot_q) + pass_on(all_wo, slot_wo)
     all_kv_sum = to_both(cross_kv, s_kv, z_kv, slot_kv)
-    ends = pass_on(all_wo, slot_wo) + pass_on(all_q, slot_q)
-    for k in (2, 3):
-        spread_on(1, k)
+    for i in (0, 1):
+        for k in (2, 3):
+            spread_on(i, k)
     out_bf[...] = (middle[...] + keep * sum_b.finish(0)).astype(jnp.bfloat16)
     local(out_bf, o_out)
     ends += all_kv_sum
@@ -1365,7 +1369,7 @@
     ]
     scratch += [(a.shape, a.dtype) for a in args[3:16]]
     for whole, parts in (
-        ((144, 512), (14, 144, 256)),
+        ((144, 512), (7, 144, 512)),
         ((160, 256), (7, 160, 256)),
         ((64, width), (14, 32, width)),
     ):

time: 260 us -> 251 us (0.965)
  Pallas kernels: 249 us -> 240 us
    pallas_call x1, Pallas kernels: 86.5 us -> 81.4 us  [feed_forward(): pl.pallas_call(ff_kernel, out_shape=(jax.ShapeDtypeStruct((tokens, width)...]
    pallas_call x1, Pallas kernels: 88.2 us -> 83.7 us  [back(): pl.pallas_call(back_kernel, out_shape=tuple((jax.ShapeDtypeStruct(*o) for...]
where the time goes in v1:
time: 251 us; the launch traced here: 247 us
  Pallas kernels  240 us (96%)
  local copies, waits for them, and re-layouts  5.03 us (2%)
    pallas_call x1, Pallas kernels, back(): pl.pallas_call(back_kernel, out_shape=tuple((jax.ShapeDtypeStruct(*o) for...  83.7 us
    pallas_call x1, Pallas kernels, feed_forward(): pl.pallas_call(ff_kernel, out_shape=(jax.ShapeDtypeStruct((tokens, width)...  81.4 us
    pallas_call x1, Pallas kernels, front(): pl.pallas_call(front_kernel, out_shape=tuple((jax.ShapeDtypeStruct(*o) fo...  64.2 us
    pallas_call x1, Pallas kernels, finish(): pl.pallas_call(finish_kernel, grid=(steps,), out_shape=[jax.ShapeDtypeStr...  10.6 us

profile of v1, /device:TPU:1, one launch (start us, length us, event | category | flops | bytes accessed | tf_op | source)
XLA Modules:
  0.0 247.2 jit_solution(7696281884455155639)
XLA Ops:
  1.3 0.7 pad.7
  2.0 0.7 pad.8
  2.6 0.7 select_select_fusion.misc
  3.3 64.2 %attention_forward.1 = (bf16[8,16,256]{2,1,0:T(8,128)(2,1)}, bf16[8,144,1536]{2,1,0:T(8,128)(2,1)}, bf16[8,128,1152]{2,1,0:T(8,128)(2,1)}, bf16[8,144,1792]{2,1,...) custom-call(bf16[192,1152]{1,0:T(8,128)(2,1)} %tokens.3, ...), custom_call_target="tpu_custom_call" | custom-call | tf_op jit(solution)/shard_map/attention_forward/pallas_call | solution.py:558
  67.5 81.4 %feed_forward.1 = (f32[192,1152]{1,0:T(8,128)}, bf16[4,2,192,1152]{3,2,1,0:T(8,128)(2,1)}, bf16[4,8,144,256]{3,2,1,0:T(8,128)(2,1)}, bf16[112,1152]{1,0:T(8,128)(2,1)}) custom-call(bf16[192,1152]{1,0:T(8,128)(2,1)} %get-tuple-element.40.own_n, bf16[4,2,192,1152]{3,2,1,0:T(8,128)(2,1)} %get-tuple-element.41.gb_all, bf16[1152,1792]{1,0:T(8,128)(2,1)} %bitcast.10, ...), custom_call_target="tpu_custom_call" | custom-call | tf_op jit(solution)/shard_map/feed_forward/pallas_call | solution.py:861
  148.9 83.7 %attention_backward.1 = (bf16[2,4,8,144,256]{4,3,2,1,0:T(8,128)(2,1)}, bf16[2,4,112,1152]{3,2,1,0:T(8,128)(2,1)}, bf16[144,1024]{1,0:T(8,128)(2,1)}, bf16[2,4,14...) custom-call(bf16[4,8,144,256]{3,2,1,0:T(8,128)(2,1)} %get-tuple-eleme, ...), custom_call_target="tpu_custom_call" | custom-call | tf_op jit(solution)/shard_map/attention_backward/pallas_call | solution.py:1387
  232.6 0.7 slice_bitcast_fusion.1
  233.3 0.8 slice_bitcast_fusion
  234.1 0.6 fusion
  234.6 0.0 copy-start.1
  234.6 0.0 copy-start
  234.6 10.6 %finish.1 = (f32[144,6912]{1,0:T(8,128)}, f32[144,6912]{1,0:T(8,128)}, f32[864,1152]{1,0:T(8,128)}, f32[144,1024]{1,0:T(8,128)}, f32[144,512]{1,0:T(8,128)}, /*index=5*/f32[128,1152]{1,0:T(8,128)}) custom-call(bf16[2,4,8,144,256]{4,3,2,1,0:T(8,128)(2,1)} %get-tuple-element.60.both, bf16[896,1152]{1,0:T(8,128)(2,1)} %bitcast.11, ...), custom_call_target="tpu_custom_call" | custom-call | tf_op jit(solution)/shard_map/finish/pallas_call | solution.py:602
  245.3 0.0 copy-done.1
  245.3 0.8 copy.25
  246.1 0.0 copy-done
  246.1 0.9 copy.26
  (3 shorter events, 0.0 us)
Async XLA Ops:
  234.6 10.6 %copy-start.1 = (bf16[192,1152]{1,0:T(8,128)(2,1)S(1)}, bf16[192,1152]{1,0:T(8,128)(2,1)}, u32[]{:S(2)}) copy-start(bf16[192,1152]{1,0:T(8,128)(2,1)} %get-tuple-element.84) | copy-start | bytes 1327108
  234.6 11.4 %copy-start = (f32[192,1152]{1,0:T(8,128)S(1)}, f32[192,1152]{1,0:T(8,128)}, u32[]{:S(2)}) copy-start(f32[192,1152]{1,0:T(8,128)} %get-tuple-element.85) | copy-start | bytes 2654212

commit v2 on v1

--- a/solution.py
+++ b/solution.py
@@ -910,9 +910,9 @@
     o_gu, o_d, o_q, o_kv, o_wo, o_out, o_grad,
     h_gu, gu_whole, z_gu, f_gu, piece_d,
     part_b, b_half, gn2, middle, miscs, x_ref, cot_ref, rope, q_ref, kv_ref, probs, att,
-    wqkv, wo, normed1, dq, r_q, q_parts, dkv, r_kv, kv_parts, dwo, r_wo, w_half,
+    wqkv, wo, normed1, dq, r_q, q_whole, q_half, q_parts, dkv, r_kv, kv_parts, dwo, r_wo, w_whole, w_half, w_parts,
     gkv, kv_out, kv_in, gproj, gmid, out_bf,
-    s_wo, y_wo, z_wo, s_q, y_q, z_q, s_kv, y_kv, z_kv,
+    s_wo, z_wo, s_q, z_q, s_kv, y_kv, z_kv,
     local_sems, send_sems, recv_sems,
 ):
     place = Place()
@@ -1086,9 +1086,10 @@
     grad_attn = (keep * grad_mid).astype(jnp.bfloat16)
     for start in range(0, width, 384):
         block = lead_product(att[...], grad_attn[:, start : start + 384]).astype(jnp.bfloat16)
-        block = block.reshape(8, 2, 64, 384)
-        dwo[0, :, :, start : start + 384] = block[:, 0]
-        dwo[1, :, :, start : start + 384] = block[:, 1]
+        block = block.reshape(8, 2, 4, 16, 384)
+        for c in range(2):
+            for q in range(4):
+                dwo[c, q, :, :, start : start + 384] = block[:, c, q]
     swap_wo = wire.copy(dwo.at[1 - core], r_wo, sibling)
     swap_wo.start()
     grad_att = trail_product(grad_attn, wo.reshape(1024, width)[...]).astype(jnp.bfloat16)
@@ -1155,40 +1156,62 @@
         kv_out[BEHIND - 1] = through.astype(jnp.bfloat16)
         pl.when(upper)(plane_kv.start)
 
+    def over_ring(blocks, whole, half):
+        return SumTree(
+            wire, over_y, RING, lambda j, p: blocks.at[core, (y + STEPS[j]) % 4], cut_lead,
+            [whole.at[0], whole.at[1], half.at[0], half.at[1]],
+        )
+
+    def near_ring(tree):
+        tree.absorb(2, 3)
+        tree.start(0, 1)
+
+    def to_owners(tree, blocks, parts):
+        tree.absorb(0, 1)
+        copies = [
+            wire.copy(blocks.at[core, y, at(j, p)], parts.at[i], device)
+            for i, ((j, p), device) in enumerate(zip(others, group))
+        ]
+        for copy in copies:
+            copy.start()
+        return copies
+
+    def to_low(copies, blocks, parts, piece, other):
+        total = blocks[core, y, me].astype(jnp.float32)
+        for i, copy in enumerate(copies):
+            copy.wait_recv()
+            total = total + parts[i].astype(jnp.float32)
+        piece[y] = total.astype(jnp.bfloat16)
+        crossing = wire.copy(piece.at[y], other, low)
+        crossing.start()
+        return crossing
+
     load_n.wait()
-    dq_rows = dq.reshape(2, width, 512)
+    dq_rows = dq.reshape(2, 4, width, 128)
     for t in range(4):
-        dq_rows[t // 2, :, 256 * (t % 2) : 256 * (t % 2 + 1)] = lead_product(
-            normed1[...], gproj[:, 256 * t : 256 * (t + 1)]
-        ).astype(jnp.bfloat16)
+        block = lead_product(normed1[...], gproj[:, 256 * t : 256 * (t + 1)]).astype(jnp.bfloat16)
+        dq_rows[t // 2, 2 * (t % 2)] = block[:, :128]
+        dq_rows[t // 2, 2 * (t % 2) + 1] = block[:, 128:]
     swap_q = wire.copy(dq.at[1 - core], r_q, sibling)
     swap_q.start()
     cross(1)
     swap_wo.wait_recv()
-    added(dwo.at[core], r_wo, 8)
-    sum_wo = SumTree(
-        wire, place.over_group, HOPS, lambda j, p: dwo.at[core, at(j, p)], cut_rows(32),
-        [w_half.at[k] for k in range(14)],
-    )
-    sum_wo.send_far()
-    sum_wo.send_mid()
-    sum_wo.start(1)
+    added(dwo.reshape(2, 32, 16, width).at[core], r_wo.reshape(32, 16, width), 32)
+    sum_wo = over_ring(dwo, w_whole, w_half)
+    sum_wo.start(2, 3)
     load_x.wait()
     load_w.wait()
     weights = wqkv.reshape(width, 1536)
     gn2[...] = trail_product(gproj[:, :1024], weights[:, :1024])
     turn(0)
     swap_q.wait_recv()
-    added(dq.at[core], r_q, 8)
-    direct_q = [
-        wire.copy(dq.at[core, at(j, p)], q_parts.at[i], device)
-        for i, ((j, p), device) in enumerate(zip(others, group))
-    ]
-    for copy in direct_q:
-        copy.start()
+    added(dq.reshape(2, 32, 144, 128).at[core], r_q.reshape(32, 144, 128), 32)
+    sum_q = over_ring(dq, q_whole, q_half)
+    sum_q.start(2, 3)
     collect_kv()
+    near_ring(sum_wo)
     turn(1)
-    sum_wo.send_near()
+    near_ring(sum_q)
     spread(0)
 
     pl.when(jnp.logical_not(upper))(plane_kv.wait_recv)
@@ -1218,8 +1241,8 @@
         dkv[1, s, 144:] = both.astype(jnp.bfloat16)
     swap_kv = wire.copy(dkv.at[1 - core], r_kv, sibling)
     swap_kv.start()
+    direct_wo = to_owners(sum_wo, dwo, w_parts)
     spread(1)
-    sum_wo.send_next()
     def over_column(source, landing):
         copies = [
             wire.copy(source.at[(y + d) % 4], landing.at[i], device)
@@ -1279,31 +1302,17 @@
     ]
     for copy in direct_kv:
         copy.start()
-    sum_wo.send_last()
+    direct_q = to_owners(sum_q, dq, q_parts)
     grad1 = grad1 * gain1
     gmid[...] += inverse1 * (grad1 - scaled1 * jnp.mean(grad1 * scaled1, axis=1, keepdims=True))
     local(gmid, o_grad)
-    total = dq[core, me].astype(jnp.float32)
-    for i, copy in enumerate(direct_q):
-        copy.wait_recv()
-        total = total + q_parts[i].astype(jnp.float32)
-    for q in range(4):
-        s_q[q] = total[:, 128 * q : 128 * (q + 1)].astype(jnp.bfloat16)
-    over_q = over_column(s_q, y_q)
     for k in (0, 1):
         arrive(tree_d, k, RING_ONWARD)
         pass_d[(2, 1)[k]].start()
-    s_wo[...] = sum_wo.finish(0).astype(jnp.bfloat16).reshape(4, 16, width)
-    over_wo = over_column(s_wo, y_wo)
+    cross_wo = to_low(direct_wo, dwo, w_parts, s_wo, z_wo)
     for k in (0, 1):
         spread_on(0, k)
-    cross_q = over_low(over_q, s_q, y_q, z_q)
-    sum_b.absorb(10)
-    sum_b.start(3)
-    sum_b.absorb(11)
-    sum_b.start(5)
-    sum_b.send_last()
-    cross_wo = over_low(over_wo, s_wo, y_wo, z_wo)
+    cross_q = to_low(direct_q, dq, q_parts, s_q, z_q)
     total = dkv[core, me].astype(jnp.float32)
     for i, copy in enumerate(direct_kv):
         copy.wait_recv()
@@ -1315,16 +1324,21 @@
     ).astype(jnp.bfloat16)
     s_kv[3] = jnp.zeros((144, 128), jnp.bfloat16)
     over_kv = over_column(s_kv, y_kv)
+    sum_b.absorb(10)
+    sum_b.start(3)
+    sum_b.absorb(11)
+    sum_b.start(5)
+    sum_b.send_last()
+    all_wo = to_all(cross_wo, s_wo, z_wo, slot_wo)
     all_q = to_all(cross_q, s_q, z_q, slot_q)
-    all_wo = to_all(cross_wo, s_wo, z_wo, slot_wo)
+    cross_kv = over_low(over_kv, s_kv, y_kv, z_kv)
     for k in (0, 1):
         spread_on(1, k)
-    cross_kv = over_low(over_kv, s_kv, y_kv, z_kv)
     for k in (2, 3):
         arrive(tree_d, k, RING_ONWARD)
     pass_d[3].start()
-    ends = pass_on(all_q, slot_q) + pass_on(all_wo, slot_wo)
     all_kv_sum = to_both(cross_kv, s_kv, z_kv, slot_kv)
+    ends = pass_on(all_wo, slot_wo) + pass_on(all_q, slot_q)
     for i in (0, 1):
         for k in (2, 3):
             spread_on(i, k)
@@ -1368,12 +1382,9 @@
         ((14, rows // 2, width), bf),
     ]
     scratch += [(a.shape, a.dtype) for a in args[3:16]]
-    for whole, parts in (
-        ((144, 512), (7, 144, 512)),
-        ((160, 256), (7, 160, 256)),
-        ((64, width), (14, 32, width)),
-    ):
-        scratch += [((2, 8, *whole), bf), ((8, *whole), bf), (parts, bf)]
+    ring = lambda *b: [(2, 4, 8, *b), (4, 8, *b), (2, 8, *b), (2, 4, *b), (7, *b)]
+    parts = ring(144, 128) + [(2, 8, 160, 256), (8, 160, 256), (7, 160, 256)] + ring(16, width)
+    scratch += [(part, bf) for part in parts]
     scratch += [
         ((BEHIND + 1, rows, 512), f32),
         ((BEHIND, rows, 512), bf),
@@ -1382,8 +1393,9 @@
         ((rows, width), f32),
         ((rows, width), bf),
     ]
-    for piece in ((16, width), (144, 128), (144, 128)):
-        scratch += [((4, *piece), bf), ((3, *piece), bf), (piece, bf)]
+    pieces = [(4, 16, width), (16, width), (4, 144, 128), (144, 128)]
+    pieces += [(4, 144, 128), (3, 144, 128), (144, 128)]
+    scratch += [(piece, bf) for piece in pieces]
     return pl.pallas_call(
         back_kernel,
         out_shape=tuple(jax.ShapeDtypeStruct(*o) for o in outs),

time: 251 us -> 244 us (0.972)
  Pallas kernels: 240 us -> 234 us
    pallas_call x1, Pallas kernels: 83.7 us -> 77.3 us  [back(): pl.pallas_call(back_kernel, out_shape=tuple((jax.ShapeDtypeStruct(*o) for...]
where the time goes in v2:
time: 244 us; the launch traced here: 241 us
  Pallas kernels  234 us (96%)
  local copies, waits for them, and re-layouts  5.03 us (2%)
    pallas_call x1, Pallas kernels, feed_forward(): pl.pallas_call(ff_kernel, out_shape=(jax.ShapeDtypeStruct((tokens, width)...  81.4 us
    pallas_call x1, Pallas kernels, back(): pl.pallas_call(back_kernel, out_shape=tuple((jax.ShapeDtypeStruct(*o) for...  77.3 us
    pallas_call x1, Pallas kernels, front(): pl.pallas_call(front_kernel, out_shape=tuple((jax.ShapeDtypeStruct(*o) fo...  64.2 us
    pallas_call x1, Pallas kernels, finish(): pl.pallas_call(finish_kernel, grid=(steps,), out_shape=[jax.ShapeDtypeStr...  10.6 us

profile of v2, /device:TPU:1, one launch (start us, length us, event | category | flops | bytes accessed | tf_op | source)
XLA Modules:
  0.0 240.8 jit_solution(6862398304591803939)
XLA Ops:
  1.3 0.7 pad.7
  2.0 0.7 pad.8
  2.6 0.7 select_select_fusion.misc
  3.3 64.2 %attention_forward.1 = (bf16[8,16,256]{2,1,0:T(8,128)(2,1)}, bf16[8,144,1536]{2,1,0:T(8,128)(2,1)}, bf16[8,128,1152]{2,1,0:T(8,128)(2,1)}, bf16[8,144,1792]{2,1,...) custom-call(bf16[192,1152]{1,0:T(8,128)(2,1)} %tokens.3, ...), custom_call_target="tpu_custom_call" | custom-call | tf_op jit(solution)/shard_map/attention_forward/pallas_call | solution.py:558
  67.5 81.4 %feed_forward.1 = (f32[192,1152]{1,0:T(8,128)}, bf16[4,2,192,1152]{3,2,1,0:T(8,128)(2,1)}, bf16[4,8,144,256]{3,2,1,0:T(8,128)(2,1)}, bf16[112,1152]{1,0:T(8,128)(2,1)}) custom-call(bf16[192,1152]{1,0:T(8,128)(2,1)} %get-tuple-element.40.own_n, bf16[4,2,192,1152]{3,2,1,0:T(8,128)(2,1)} %get-tuple-element.41.gb_all, bf16[1152,1792]{1,0:T(8,128)(2,1)} %bitcast.10, ...), custom_call_target="tpu_custom_call" | custom-call | tf_op jit(solution)/shard_map/feed_forward/pallas_call | solution.py:861
  148.9 77.3 %attention_backward.1 = (bf16[2,4,8,144,256]{4,3,2,1,0:T(8,128)(2,1)}, bf16[2,4,112,1152]{3,2,1,0:T(8,128)(2,1)}, bf16[144,1024]{1,0:T(8,128)(2,1)}, bf16[2,4,14...) custom-call(bf16[4,8,144,256]{3,2,1,0:T(8,128)(2,1)} %get-tuple-eleme, ...), custom_call_target="tpu_custom_call" | custom-call | tf_op jit(solution)/shard_map/attention_backward/pallas_call | solution.py:1399
  226.2 0.7 slice_bitcast_fusion.1
  226.9 0.8 slice_bitcast_fusion
  227.7 0.6 fusion
  228.3 0.0 copy-start.1
  228.3 0.0 copy-start
  228.3 10.6 %finish.1 = (f32[144,6912]{1,0:T(8,128)}, f32[144,6912]{1,0:T(8,128)}, f32[864,1152]{1,0:T(8,128)}, f32[144,1024]{1,0:T(8,128)}, f32[144,512]{1,0:T(8,128)}, /*index=5*/f32[128,1152]{1,0:T(8,128)}) custom-call(bf16[2,4,8,144,256]{4,3,2,1,0:T(8,128)(2,1)} %get-tuple-element.60.both, bf16[896,1152]{1,0:T(8,128)(2,1)} %bitcast.11, ...), custom_call_target="tpu_custom_call" | custom-call | tf_op jit(solution)/shard_map/finish/pallas_call | solution.py:602
  238.9 0.0 copy-done.1
  238.9 0.8 copy.25
  239.7 0.0 copy-done
  239.7 0.9 copy.26
  (3 shorter events, 0.0 us)
Async XLA Ops:
  228.3 10.6 %copy-start.1 = (bf16[192,1152]{1,0:T(8,128)(2,1)S(1)}, bf16[192,1152]{1,0:T(8,128)(2,1)}, u32[]{:S(2)}) copy-start(bf16[192,1152]{1,0:T(8,128)(2,1)} %get-tuple-element.84) | copy-start | bytes 1327108
  228.3 11.4 %copy-start = (f32[192,1152]{1,0:T(8,128)S(1)}, f32[192,1152]{1,0:T(8,128)}, u32[]{:S(2)}) copy-start(f32[192,1152]{1,0:T(8,128)} %get-tuple-element.85) | copy-start | bytes 2654212

commit v3 on v2

--- a/solution.py
+++ b/solution.py
@@ -194,7 +194,7 @@
     tokens, cot, misc, freq, w_query, w_keyval, w_out, w_gate, w_up,
     o_misc, o_qkv, o_wo, o_gu, o_gb, o_normed1, o_q, o_kv, o_probs, o_att, o_middle, o_normed2, o_rope,
     x_ref, cot_ref, miscs, freq_ref, wqkv, wo, gate, up, packed, gb_own, normed1, q_ref, kv_ref,
-    bias, probs, att, middle, normed2, rope,
+    bias, probs, att, middle, normed2, rope, wo_own,
     local_sems, send_sems, recv_sems,
 ):
     place = Place()
@@ -224,7 +224,7 @@
     load_own = [
         local(w_query, wqkv.at[me, :, pl.ds(0, 1024)]),
         local(w_keyval, wqkv.at[me, :, pl.ds(1024, 512)]),
-        local(w_out, wo.at[me]),
+        local(w_out, wo_own),
     ]
     greet([sibling] + group + [d for d, (j, p) in zip(sequence, others) if p == 1] + column)
 
@@ -248,7 +248,6 @@
 
     cut_q, cut_kv = lanes_from(0, 512), lanes_from(1024, 256)
     slot_qkv = lambda j, p: wqkv.at[at(j, p)]
-    slot_wo = lambda j, p: wo.at[at(j, p)]
     slot_gb = lambda j, p: o_gb.at[j, p]
     misc_copies = [wire.copy(misc, miscs.at[me], device) for device in sequence]
     for copy in misc_copies:
@@ -259,10 +258,9 @@
     trees = [
         gather_tree(wire, place.over_group, HOPS, own, slot_qkv, cut_q, True),
         gather_tree(wire, place.over_group, HOPS, own, slot_qkv, cut_kv, True),
-        gather_tree(wire, place.over_group, HOPS, wo.at[me], slot_wo, cut_wo, True),
-    ]
-    cuts = [cut_q, cut_kv, cut_wo]
-    slots = [slot_qkv, slot_qkv, slot_wo]
+    ]
+    cuts = [cut_q, cut_kv]
+    slots = [slot_qkv, slot_qkv]
     passes = [
         {k: wire.copy(cut(slot(*jp), 0), cut(slot(*jp), 0), sibling) for k, jp in WHOLE.items()}
         for cut, slot in zip(cuts, slots)
@@ -311,6 +309,14 @@
         cut_gu(packed.at[me]), cut_gu(o_gu.at[me]), local_sems.at[len(locals_)]
     )
     locals_.append(None)
+    held_wo = lambda j, p: cut_wo(wo.at[shard_from(STEPS[j], p)], 0)
+    turn_wo = wire.copy(cut_wo(wo_own, 0), cut_wo(wo.at[me], 0), place.device(dx=4 - y))
+    keep_wo = pltpu.make_async_copy(
+        cut_wo(wo_own, 0), cut_wo(wo.at[me], 0), local_sems.at[len(locals_)]
+    )
+    locals_.append(None)
+    pl.when(away)(turn_wo.start)
+    pl.when(home)(keep_wo.start)
     turn[1].start()
     pl.when(away)(turn[0].start)
     pl.when(home)(keep_own.start)
@@ -336,6 +342,27 @@
         for p in (0, 1)
     }
 
+    wo_slots = [lambda j, _, p=p: wo.at[shard_from(STEPS[j], p)] for p in (0, 1)]
+    wo_trees = [
+        gather_tree(wire, over_y, RING, slot(0, 0), slot, cut_wo, True) for slot in wo_slots
+    ]
+    mirror_wo = wire.copy(held_wo(0, 0), held_wo(0, 0), place.device(mirror=1))
+    wo_passes = {
+        (j, p): wire.copy(held_wo(j, p), held_wo(j, p), sibling)
+        for j in range(4)
+        for p in (0, 1)
+    }
+
+    def start_wo(p):
+        for copy in (wo_trees[p][0], wo_trees[p][1], wo_passes[0, p]):
+            copy.start()
+
+    def over_wo(k, j):
+        for p in (0, 1):
+            arrive(wo_trees[p], k, RING_ONWARD)
+            if j:
+                wo_passes[j, p].start()
+
     def over(k, j):
         for p in (0, 1):
             arrive(gu_trees[p], k, RING_ONWARD)
@@ -352,7 +379,13 @@
     )
     gb_own[...] = jnp.where(live_col, cot_ref[...].astype(jnp.float32), 0.0).astype(jnp.bfloat16)
     gb_tree = gather_tree(wire, place.over_group, HOPS, gb_own, slot_gb, cut_gb, False)
+    pl.when(away)(turn_wo.wait_recv)
+    pl.when(home)(keep_wo.wait)
+    mirror_wo.start()
+    start_wo(0)
     attn(3, 11, 6)
+    mirror_wo.wait_recv()
+    start_wo(1)
     pl.when(away)(turn[0].wait_recv)
     turn[1].wait_recv()
     pl.when(home)(keep_own.wait)
@@ -448,6 +481,8 @@
     bias[...] = jnp.where(allowed, 0.0, MASKED)
     pass_kv()
 
+    over_wo(0, 2)
+    over_wo(1, 1)
     over(0, 2)
     over(1, 1)
     for k in SERVE[:4]:
@@ -465,8 +500,10 @@
         if h == 1:
             for k in SERVE[4:6]:
                 arrive(gb_tree, k)
-    for k in WHOLE:
-        passes[2][k].wait_recv()
+    over_wo(2, 0)
+    over_wo(3, 3)
+    for copy in wo_passes.values():
+        copy.wait_recv()
     keep = jnp.where(live_col, 1.0, 0.0)
     mid = x_ref[...].astype(jnp.float32) + keep * matmul(att[...], wo.reshape(1024, width)[...])
     middle[...] = mid
@@ -492,11 +529,12 @@
         arrive(gb_tree, k)
     for copy in gu_passes.values():
         copy.wait_recv()
-    waited = [id(copy) for copy in near_kv + far_kv + [cross_kv, turn[0]]]
+    waited = [id(copy) for copy in near_kv + far_kv + [cross_kv, turn[0], turn_wo]]
     for copy in locals_[9:]:
         if copy is not None:
             copy.wait()
     pl.when(away)(turn[0].wait_send)
+    pl.when(away)(turn_wo.wait_send)
     pl.when(jnp.logical_not(upper))(cross_kv.wait_send)
     for i, (near, far) in enumerate(zip(near_kv, far_kv)):
         pl.when(x + (i + 1) < 4)(near.wait_send)
@@ -554,6 +592,7 @@
         ((rows, width), f32),
         ((rows, width), bf),
         ((rows, 256), f32),
+        (w_out.shape, bf),
     ]
     return pl.pallas_call(
         front_kernel,

time: 244 us -> 240 us (0.984)
  Pallas kernels: 234 us -> 230 us
    pallas_call x1, Pallas kernels: 81.4 us -> 70.3 us  [feed_forward(): pl.pallas_call(ff_kernel, out_shape=(jax.ShapeDtypeStruct((tokens, width)...]
    pallas_call x1, Pallas kernels: 64.2 us -> 69.2 us  [front(): pl.pallas_call(front_kernel, out_shape=tuple((jax.ShapeDtypeStruct(*o) fo...]
where the time goes in v3:
time: 240 us; the launch traced here: 237 us
  Pallas kernels  230 us (96%)
  local copies, waits for them, and re-layouts  5.03 us (2%)
    pallas_call x1, Pallas kernels, back(): pl.pallas_call(back_kernel, out_shape=tuple((jax.ShapeDtypeStruct(*o) for...  79.4 us
    pallas_call x1, Pallas kernels, feed_forward(): pl.pallas_call(ff_kernel, out_shape=(jax.ShapeDtypeStruct((tokens, width)...  70.3 us
    pallas_call x1, Pallas kernels, front(): pl.pallas_call(front_kernel, out_shape=tuple((jax.ShapeDtypeStruct(*o) fo...  69.2 us
    pallas_call x1, Pallas kernels, finish(): pl.pallas_call(finish_kernel, grid=(steps,), out_shape=[jax.ShapeDtypeStr...  10.6 us

profile of v3, /device:TPU:1, one launch (start us, length us, event | category | flops | bytes accessed | tf_op | source)
XLA Modules:
  0.0 236.8 jit_solution(617882173355003786)
XLA Ops:
  1.3 0.7 pad.7
  2.0 0.7 pad.8
  2.6 0.7 select_select_fusion.misc
  3.3 69.2 %attention_forward.1 = (bf16[8,16,256]{2,1,0:T(8,128)(2,1)}, bf16[8,144,1536]{2,1,0:T(8,128)(2,1)}, bf16[8,128,1152]{2,1,0:T(8,128)(2,1)}, bf16[8,144,1792]{2,1,...) custom-call(bf16[192,1152]{1,0:T(8,128)(2,1)} %tokens.3, ...), custom_call_target="tpu_custom_call" | custom-call | tf_op jit(solution)/shard_map/attention_forward/pallas_call | solution.py:597
  72.5 70.3 %feed_forward.1 = (f32[192,1152]{1,0:T(8,128)}, bf16[4,2,192,1152]{3,2,1,0:T(8,128)(2,1)}, bf16[4,8,144,256]{3,2,1,0:T(8,128)(2,1)}, bf16[112,1152]{1,0:T(8,128)(2,1)}) custom-call(bf16[192,1152]{1,0:T(8,128)(2,1)} %get-tuple-element.40.own_n, bf16[4,2,192,1152]{3,2,1,0:T(8,128)(2,1)} %get-tuple-element.41.gb_all, bf16[1152,1792]{1,0:T(8,128)(2,1)} %bitcast.10, ...), custom_call_target="tpu_custom_call" | custom-call | tf_op jit(solution)/shard_map/feed_forward/pallas_call | solution.py:900
  142.9 79.4 %attention_backward.1 = (bf16[2,4,8,144,256]{4,3,2,1,0:T(8,128)(2,1)}, bf16[2,4,112,1152]{3,2,1,0:T(8,128)(2,1)}, bf16[144,1024]{1,0:T(8,128)(2,1)}, bf16[2,4,14...) custom-call(bf16[4,8,144,256]{3,2,1,0:T(8,128)(2,1)} %get-tuple-eleme, ...), custom_call_target="tpu_custom_call" | custom-call | tf_op jit(solution)/shard_map/attention_backward/pallas_call | solution.py:1438
  222.2 0.7 slice_bitcast_fusion.1
  222.9 0.8 slice_bitcast_fusion
  223.7 0.6 fusion
  224.3 0.0 copy-start.1
  224.3 0.0 copy-start
  224.3 10.6 %finish.1 = (f32[144,6912]{1,0:T(8,128)}, f32[144,6912]{1,0:T(8,128)}, f32[864,1152]{1,0:T(8,128)}, f32[144,1024]{1,0:T(8,128)}, f32[144,512]{1,0:T(8,128)}, /*index=5*/f32[128,1152]{1,0:T(8,128)}) custom-call(bf16[2,4,8,144,256]{4,3,2,1,0:T(8,128)(2,1)} %get-tuple-element.60.both, bf16[896,1152]{1,0:T(8,128)(2,1)} %bitcast.11, ...), custom_call_target="tpu_custom_call" | custom-call | tf_op jit(solution)/shard_map/finish/pallas_call | solution.py:641
  234.9 0.0 copy-done.1
  234.9 0.8 copy.25
  235.7 0.0 copy-done
  235.7 0.9 copy.26
  (3 shorter events, 0.0 us)
Async XLA Ops:
  224.3 10.6 %copy-start.1 = (bf16[192,1152]{1,0:T(8,128)(2,1)S(1)}, bf16[192,1152]{1,0:T(8,128)(2,1)}, u32[]{:S(2)}) copy-start(bf16[192,1152]{1,0:T(8,128)(2,1)} %get-tuple-element.84) | copy-start | bytes 1327108
  224.3 11.4 %copy-start = (f32[192,1152]{1,0:T(8,128)S(1)}, f32[192,1152]{1,0:T(8,128)}, u32[]{:S(2)}) copy-start(f32[192,1152]{1,0:T(8,128)} %get-tuple-element.85) | copy-start | bytes 2654212

commit v4 on v3

--- a/solution.py
+++ b/solution.py
@@ -633,9 +633,10 @@
 
 def finish(both, d_in, q_in, kv_in, wo_in):
     rows, width = both.shape[3], d_in.shape[1]
-    steps = rows // 16
+    tall = 48
+    steps = rows // tall
     shapes = [(rows, 8 * FF_DEV)] * 2 + [(FF_DEV, width), (rows, 1024), (rows, 512), wo_in.shape]
-    blocks = [(16, 8 * FF_DEV)] * 2 + [(FF_DEV // steps, width), (16, 1024), (16, 512)]
+    blocks = [(tall, 8 * FF_DEV)] * 2 + [(FF_DEV // steps, width), (tall, 1024), (tall, 512)]
     by_row = lambda i: (i, 0)
     fixed = pl.BlockSpec(wo_in.shape, lambda i: (0, 0))
     return pl.pallas_call(
@@ -643,10 +644,10 @@
         grid=(steps,),
         out_shape=[jax.ShapeDtypeStruct(shape, jnp.float32) for shape in shapes],
         in_specs=[
-            pl.BlockSpec((2, 4, 8, 16, 256), lambda i: (0, 0, 0, i, 0)),
+            pl.BlockSpec((2, 4, 8, tall, 256), lambda i: (0, 0, 0, i, 0)),
             pl.BlockSpec((FF_DEV // steps, width), by_row),
-            pl.BlockSpec((16, 1024), by_row),
-            pl.BlockSpec((2, 4, 16, 128), lambda i: (0, 0, i, 0)),
+            pl.BlockSpec((tall, 1024), by_row),
+            pl.BlockSpec((2, 4, tall, 128), lambda i: (0, 0, i, 0)),
             fixed,
         ],
         out_specs=[pl.BlockSpec(block, by_row) for block in blocks] + [fixed],

time: 240 us -> 238 us (level)
  Pallas kernels: 230 us -> 227 us
where the time goes in v4:
time: 238 us; the launch traced here: 235 us
  Pallas kernels  227 us (95%)
  local copies, waits for them, and re-layouts  5.03 us (2%)
    pallas_call x1, Pallas kernels, back(): pl.pallas_call(back_kernel, out_shape=tuple((jax.ShapeDtypeStruct(*o) for...  79.4 us
    pallas_call x1, Pallas kernels, feed_forward(): pl.pallas_call(ff_kernel, out_shape=(jax.ShapeDtypeStruct((tokens, width)...  70.3 us
    pallas_call x1, Pallas kernels, front(): pl.pallas_call(front_kernel, out_shape=tuple((jax.ShapeDtypeStruct(*o) fo...  69.2 us
    pallas_call x1, Pallas kernels, finish(): pl.pallas_call(finish_kernel, grid=(steps,), out_shape=[jax.ShapeDtypeStr...  8.49 us

profile of v4, /device:TPU:1, one launch (start us, length us, event | category | flops | bytes accessed | tf_op | source)
XLA Modules:
  0.0 234.7 jit_solution(1048895001285735434)
XLA Ops:
  1.3 0.7 pad.7
  2.0 0.7 pad.8
  2.6 0.7 select_select_fusion.misc
  3.3 69.2 %attention_forward.1 = (bf16[8,16,256]{2,1,0:T(8,128)(2,1)}, bf16[8,144,1536]{2,1,0:T(8,128)(2,1)}, bf16[8,128,1152]{2,1,0:T(8,128)(2,1)}, bf16[8,144,1792]{2,1,...) custom-call(bf16[192,1152]{1,0:T(8,128)(2,1)} %tokens.3, ...), custom_call_target="tpu_custom_call" | custom-call | tf_op jit(solution)/shard_map/attention_forward/pallas_call | solution.py:597
  72.5 70.3 %feed_forward.1 = (f32[192,1152]{1,0:T(8,128)}, bf16[4,2,192,1152]{3,2,1,0:T(8,128)(2,1)}, bf16[4,8,144,256]{3,2,1,0:T(8,128)(2,1)}, bf16[112,1152]{1,0:T(8,128)(2,1)}) custom-call(bf16[192,1152]{1,0:T(8,128)(2,1)} %get-tuple-element.40.own_n, bf16[4,2,192,1152]{3,2,1,0:T(8,128)(2,1)} %get-tuple-element.41.gb_all, bf16[1152,1792]{1,0:T(8,128)(2,1)} %bitcast.10, ...), custom_call_target="tpu_custom_call" | custom-call | tf_op jit(solution)/shard_map/feed_forward/pallas_call | solution.py:901
  142.9 79.4 %attention_backward.1 = (bf16[2,4,8,144,256]{4,3,2,1,0:T(8,128)(2,1)}, bf16[2,4,112,1152]{3,2,1,0:T(8,128)(2,1)}, bf16[144,1024]{1,0:T(8,128)(2,1)}, bf16[2,4,14...) custom-call(bf16[4,8,144,256]{3,2,1,0:T(8,128)(2,1)} %get-tuple-eleme, ...), custom_call_target="tpu_custom_call" | custom-call | tf_op jit(solution)/shard_map/attention_backward/pallas_call | solution.py:1439
  222.2 0.7 slice_bitcast_fusion.1
  222.9 0.8 slice_bitcast_fusion
  223.7 0.6 fusion
  224.3 0.0 copy-start.1
  224.3 0.0 copy-start
  224.3 8.5 %finish.1 = (f32[144,6912]{1,0:T(8,128)}, f32[144,6912]{1,0:T(8,128)}, f32[864,1152]{1,0:T(8,128)}, f32[144,1024]{1,0:T(8,128)}, f32[144,512]{1,0:T(8,128)}, /*index=5*/f32[128,1152]{1,0:T(8,128)}) custom-call(bf16[2,4,8,144,256]{4,3,2,1,0:T(8,128)(2,1)} %get-tuple-element.60.both, bf16[896,1152]{1,0:T(8,128)(2,1)} %bitcast.11, ...), custom_call_target="tpu_custom_call" | custom-call | tf_op jit(solution)/shard_map/finish/pallas_call | solution.py:642
  232.8 0.0 copy-done.1
  232.8 0.8 copy.25
  233.6 0.0 copy-done
  233.6 0.9 copy.26
  (3 shorter events, 0.0 us)
Async XLA Ops:
  224.3 8.5 %copy-start.1 = (bf16[192,1152]{1,0:T(8,128)(2,1)S(1)}, bf16[192,1152]{1,0:T(8,128)(2,1)}, u32[]{:S(2)}) copy-start(bf16[192,1152]{1,0:T(8,128)(2,1)} %get-tuple-element.84) | copy-start | bytes 1327108
  224.3 9.3 %copy-start = (f32[192,1152]{1,0:T(8,128)S(1)}, f32[192,1152]{1,0:T(8,128)}, u32[]{:S(2)}) copy-start(f32[192,1152]{1,0:T(8,128)} %get-tuple-element.85) | copy-start | bytes 2654212
